TPU v7x, 32 devices: a whole 2x2x4 slice. The times are simulated.
32 devices in a mesh: grp: 1, seq: 8 (over z, y), head: 4 (over x, core).
Axes of the slice: x: 2, y: 2, z: 4, core: 2. Of those that a mesh axis runs over, the one named last changes fastest.
Arguments:
- ssm_values: bfloat16 [2048, 4096], P(('grp', 'seq'), 'head'), may hold values from -6 to 6
- ssm_gate: bfloat16 [2048, 4096], P(('grp', 'seq'), 'head'), may hold values from -6 to 6
- write_proj: bfloat16 [2048, 1024], P(('grp', 'seq'), 'head'), may hold values from -2.5 to 2.5
- read_proj: bfloat16 [2048, 1024], P(('grp', 'seq'), 'head'), may hold values from -2.5 to 2.5
- step_size: float32 [2048, 64], P(('grp', 'seq'), 'head'), may hold values from 0.003125 to 0.2
- decay_power: int32 [64], P('head'), may hold values from 0 to 15
- skip_gain: float32 [64], P('head'), may hold values from 0.5 to 1.5
- norm_gain: float32 [4096], P('head'), may hold values from 0.1 to 1.9
- out_weight: bfloat16 [4096, 2688], P('head', 'seq'), may hold values from -0.09375 to 0.09375
- residual: bfloat16 [2048, 2688], P(('grp', 'seq', 'head')), may hold values from -6 to 6
- expert_norm: float32 [2688], replicated, may hold values from 0.1 to 1.9
- router_weight: bfloat16 [2688, 16], replicated, may hold values from -0.125 to 0.125
- expert_index: int32 [2048, 6], P(('grp', 'seq', 'head')), may hold values from 0 to 15, all different within a row; in each aligned block of 64 rows (0 to 63, 64 to 127, ...) at most 32 rows name the same one
- up_weight: bfloat16 [32, 2688, 928], P(('seq', 'head')), may hold values from -0.125 to 0.125
- down_weight: bfloat16 [32, 928, 2688], P(('seq', 'head')), may hold values from -0.125 to 0.125
Outputs:
- layer_out: bfloat16 [2048, 2688], P(('grp', 'seq', 'head'))
Inputs may be any that keep to these rules, and one draw needn't show every extreme that they name: `expert_index`: each row names 6 different experts. In the rows of one device (aligned blocks of 64 rows) no expert is named more than 32 times, a bound that some block reaches.
All inputs are finite; a program needn't handle non-finite values.
Results may differ from a plain program's by a relative error of at most 0.019.
Values may be sent and summed in bfloat16 or wider, within the bound.
A program may use at most 64 MiB of HBM per device.

v0:
```python
import jax
import jax.numpy as jnp
from jax import lax
from jax.sharding import PartitionSpec as P

HEADS = 64
HEAD_DIM = 64
STATE = 128
GROUPS = 8
TOP = 6
BLOCK_LEN = 256


EPSILON = 1e-05
ROUTE_SCALE = 2.5


def entering(x, axis, combine, identity):
    size, mine = (lax.axis_size(axis), lax.axis_index(axis))
    everything = jax.tree.map(
        lambda part, kind: lax.all_gather(part.astype(kind), axis), x, (jnp.bfloat16, jnp.bfloat16)
    )
    start = jax.tree.map(
        lambda part, zero: jnp.broadcast_to(jnp.asarray(zero, part.dtype), part.shape), x, identity
    )

    def turn(k, before):
        reached = k < mine
        new = combine(
            before, jax.tree.map(lambda part, own: part[k].astype(own.dtype), everything, x)
        )
        return jax.tree.map(lambda a, b: jnp.where(reached, a, b), new, before)

    return lax.fori_loop(0, size, turn, start)


def partner(x, axis, stride):
    return lax.ppermute(x, axis, [(i, i ^ 1 << stride) for i in range(lax.axis_size(axis))])


def expert_half(slot_rows, up_weight, down_weight):
    model_width = slot_rows.shape[-1]
    flat_rows = slot_rows.reshape(-1, model_width)
    activation = jnp.dot(flat_rows, up_weight[0], preferred_element_type=jnp.float32)
    activation = jnp.maximum(activation, 0.0)
    activation = (activation * activation).astype(jnp.bfloat16)
    output = jnp.dot(activation, down_weight[0], preferred_element_type=jnp.float32).astype(
        jnp.bfloat16
    )
    return output.reshape(slot_rows.shape)


def per_device(
    ssm_values,
    ssm_gate,
    write_proj,
    read_proj,
    step_size,
    decay_power,
    skip_gain,
    norm_gain,
    out_weight,
    residual,
    expert_norm,
    router_weight,
    expert_index,
    up_weight,
    down_weight,
):
    tokens_dev = ssm_values.shape[0]
    heads_dev = step_size.shape[1]
    per_group = HEADS // GROUPS
    groups_dev = heads_dev // per_group
    count_blocks = tokens_dev // BLOCK_LEN
    decay_rates = jnp.exp2(-decay_power.astype(jnp.float32))
    values = ssm_values.reshape(count_blocks, BLOCK_LEN, heads_dev, HEAD_DIM)
    steps_all = step_size.reshape(count_blocks, BLOCK_LEN, heads_dev)
    writes = write_proj.reshape(count_blocks, BLOCK_LEN, groups_dev, STATE)
    reads = read_proj.reshape(count_blocks, BLOCK_LEN, groups_dev, STATE)
    causal = jnp.tril(jnp.ones((BLOCK_LEN, BLOCK_LEN), dtype=bool))

    def one_block(pieces):
        values_in, steps_in, write_in, read_in = pieces
        log_decay = -steps_in * decay_rates[None, :]
        cumulative = jnp.cumsum(log_decay, axis=0)
        scores = jnp.einsum("tgn,sgn->gts", read_in, write_in, preferred_element_type=jnp.float32)
        scores = jnp.repeat(scores, per_group, axis=0)
        decays = jnp.exp(cumulative.T[:, :, None] - cumulative.T[:, None, :])
        mixing = jnp.where(causal[None], scores * decays * steps_in.T[:, None, :], 0.0).astype(
            jnp.bfloat16
        )
        inner_out = jnp.einsum(
            "hts,shp->thp", mixing, values_in, preferred_element_type=jnp.float32
        )
        block_total = cumulative[-1]
        weighted = (
            values_in.astype(jnp.float32)
            * (jnp.exp(block_total[None, :] - cumulative) * steps_in)[:, :, None]
        ).astype(jnp.bfloat16)
        write_heads = jnp.repeat(write_in, per_group, axis=1)
        fresh_state = jnp.einsum(
            "shp,shn->hpn", weighted, write_heads, preferred_element_type=jnp.float32
        )
        return (inner_out, fresh_state, block_total, cumulative)

    inner_all, fresh_all, totals_blk, cumul_all = lax.map(
        one_block, (values, steps_all, writes, reads)
    )

    def summarize(carried_in, pieces):
        decay_prod, summary = carried_in
        block_total, fresh_state = pieces
        factor = jnp.exp(block_total)
        return ((decay_prod * factor, factor[:, None, None] * summary + fresh_state), None)

    zero_state = jnp.zeros((heads_dev, HEAD_DIM, STATE), jnp.float32)
    (device_decay, device_state), unused = lax.scan(
        summarize, (jnp.ones((heads_dev,), jnp.float32), zero_state), (totals_blk, fresh_all)
    )

    def combine(earlier, later):
        return (earlier[0] * later[0], later[0][:, None, None] * earlier[1] + later[1])

    identity = (jnp.ones_like(device_decay), jnp.zeros_like(device_state))
    prior_decay, incoming = entering((device_decay, device_state), "seq", combine, identity)

    def emit_rows(carry_state, pieces):
        read_in, cumulative, block_total, fresh_state = pieces
        read_heads = jnp.repeat(read_in, per_group, axis=1)
        carried = jnp.einsum(
            "thn,hpn->thp",
            read_heads,
            carry_state.astype(jnp.bfloat16),
            preferred_element_type=jnp.float32,
        )
        carried = carried * jnp.exp(cumulative)[:, :, None]
        return (jnp.exp(block_total)[:, None, None] * carry_state + fresh_state, carried)

    final_state, carried_all = lax.scan(
        emit_rows, incoming, (reads, cumul_all, totals_blk, fresh_all)
    )
    values_flat = ssm_values.reshape(tokens_dev, heads_dev, HEAD_DIM).astype(jnp.float32)
    ssm_out = (inner_all + carried_all).reshape(tokens_dev, heads_dev, HEAD_DIM) + skip_gain[
        None, :, None
    ] * values_flat
    gate_vals = ssm_gate.reshape(tokens_dev, heads_dev, HEAD_DIM).astype(jnp.float32)
    gated = (ssm_out * jax.nn.silu(gate_vals)).reshape(tokens_dev, groups_dev, per_group * HEAD_DIM)
    inv_rms = lax.rsqrt(jnp.mean(gated * gated, axis=-1, keepdims=True) + EPSILON)
    normed = (
        (gated * inv_rms).reshape(tokens_dev, heads_dev * HEAD_DIM) * norm_gain[None, :]
    ).astype(jnp.bfloat16)
    weight_full = lax.all_gather(out_weight, "seq", axis=1, tiled=True)
    rows_own = tokens_dev // lax.axis_size("head")
    mixed_out = lax.psum_scatter(
        jnp.dot(normed, weight_full, preferred_element_type=jnp.float32).astype(jnp.bfloat16),
        "head",
        scatter_dimension=0,
        tiled=True,
    ).astype(jnp.float32)
    hidden = residual.astype(jnp.float32) + mixed_out
    inputs = (
        hidden
        * lax.rsqrt(jnp.mean(hidden * hidden, axis=-1, keepdims=True) + EPSILON)
        * expert_norm[None, :]
    ).astype(jnp.bfloat16)
    logits = jnp.dot(inputs, router_weight, preferred_element_type=jnp.float32)
    experts = router_weight.shape[1]
    model_width = inputs.shape[1]
    expert_hits = expert_index[:, :, None] == jnp.arange(experts, dtype=jnp.int32)[None, None, :]
    picked = jnp.sum(jnp.where(expert_hits, logits[:, None, :], 0.0), axis=-1)
    probability = jax.nn.sigmoid(picked)
    shares = ROUTE_SCALE * probability / jnp.sum(probability, axis=1, keepdims=True)
    capacity = (
        8
        * TOP
        * tokens_dev
        // (3 * lax.axis_size("seq") * lax.axis_size("head") * lax.axis_size("head"))
    )
    flat_hits = expert_hits.astype(jnp.int32).reshape(rows_own * TOP, experts)
    before = jnp.cumsum(flat_hits, axis=0) - flat_hits
    slot_index = jnp.sum(before * flat_hits, axis=1)
    target = expert_index.reshape(rows_own * TOP) * capacity + slot_index
    placing = jnp.arange(experts * capacity, dtype=jnp.int32)[:, None] == target[None, :]
    placing = jnp.any(placing.reshape(experts * capacity, rows_own, TOP), axis=2).astype(
        jnp.bfloat16
    )
    outgoing = jnp.dot(placing, inputs, preferred_element_type=jnp.float32).astype(jnp.bfloat16)
    outgoing = outgoing.reshape(experts, capacity, model_width)
    halves = outgoing.reshape(experts, 2, capacity // 2, model_width).reshape(
        2 * experts, capacity // 2, model_width
    )
    slot_rows = lax.all_to_all(halves, ("seq", "head"), split_axis=0, concat_axis=0, tiled=True)
    other_rows = partner(slot_rows, "head", 0)
    both_rows = jnp.concatenate([slot_rows, other_rows], axis=1)
    both_parts = expert_half(both_rows, up_weight, down_weight)
    own_part = both_parts[:, : slot_rows.shape[1]]
    other_part = both_parts[:, slot_rows.shape[1] :]
    back_part = partner(other_part, "head", 0)
    summed = (own_part.astype(jnp.float32) + back_part.astype(jnp.float32)).astype(jnp.bfloat16)
    returned = lax.all_to_all(summed, ("seq", "head"), split_axis=0, concat_axis=0, tiled=True)
    results = returned.reshape(experts, 2, capacity // 2, model_width).reshape(
        experts, capacity, model_width
    )
    gathered = results.reshape(experts * capacity, model_width)[target].reshape(
        rows_own, TOP, model_width
    )
    moe_out = jnp.sum(shares[:, :, None] * gathered.astype(jnp.float32), axis=1)
    return (hidden + moe_out).astype(jnp.bfloat16)


def solution(mesh):
    return jax.shard_map(
        per_device,
        mesh=mesh,
        in_specs=(
            P(("grp", "seq"), "head"),
            P(("grp", "seq"), "head"),
            P(("grp", "seq"), "head"),
            P(("grp", "seq"), "head"),
            P(("grp", "seq"), "head"),
            P("head"),
            P("head"),
            P("head"),
            P("head", "seq"),
            P(("grp", "seq", "head"), None),
            P(),
            P(),
            P(("grp", "seq", "head"), None),
            P(("seq", "head"), None, None),
            P(("seq", "head"), None, None),
        ),
        out_specs=P(("grp", "seq", "head"), None),
        check_vma=False,
    )
```

profile of v0, /device:TPU:0, one launch (start us, length us, event | category | flops | bytes accessed | tf_op | source)
XLA Modules:
  0.0 379.4 jit_solution(6927901179226233715)
XLA Ops:
  6.6 0.7 multiply_exponential_fusion
  7.3 0.8 copy_bitcast_fusion.3
  8.1 0.6 reduce-window.14
  9.1 0.8 exponential_multiply_fusion
  10.0 1.2 copy.62
  11.3 0.2 broadcast_in_dim.95
  11.5 1.0 fusion.11
  12.5 0.7 all-gather.5.cloned.1.call-update
  13.5 22.2 %all-gather.1 = bf16[8,1,16]{2,1,0:T(2,128)(2,1)S(1)} all-gather(bf16[1,1,16]{2,1,0:T(2,128)(2,1)S(1)} %bitcast.150), channel_id=1, replica_groups=mesh['grp'=1,'seq'=8,'head'=4] {'seq'}, dimensions={0}, use_global_device_ids=true | all-gather | bytes 288 | tf_op jit(solution)/shard_map/all_gather | solution.py:21
  35.7 0.2 copy.66
  36.2 0.2 fusion.35
  36.4 1.2 fusion.6
  37.6 0.8 convolution_bitcast_fusion
  38.4 26.3 %all-gather.7.cloned.1.call-done = bf16[128,64,128]{2,1,0:T(8,128)(2,1)} async-done(((bf16[16,64,128]{2,1,0:T(8,128)(2,1)}), bf16[128,64,128]{2,1,0:T(8,128)(2,1)}) %all-gather.7.cloned.1.call-update) | async-done | bytes 2097168 | tf_op jit(solution)/shard_map/all_gather | solution.py:21
  64.6 9.1 %while.9 = (s32[]{:T(128)}, f32[16,64,128]{2,1,0:T(8,128)S(1)}, s32[]{:T(128)}, bf16[8,16]{1,0:T(8,128)(2,1)S(1)}, bf16[8,16,64,128]{3,2,1,0:T(8,128)(2,1)}, /*index=5*/s32[]{:T(128)}, s32[]{:T(128)}) while((s32[]{:T(128)}, f32[16,64,128]{2,1,0:T(8,128)S(1)}, s32[]{:T(128)}, bf16[8,16]{1,0:T(8,128)(2,1)S(1)}, ...), condition=%wide.region_3.4_spmd.clone, body=%wide.region_2.3_spmd.clone.sunk | while | flops 655380 | bytes 1310985 | solution.py:34
  64.6 1.1 fusion.61
  65.8 1.1 fusion.61
  66.9 1.1 fusion.61
  68.0 1.1 fusion.61
  69.2 1.1 fusion.61
  70.3 1.1 fusion.61
  71.4 1.1 fusion.61
  72.6 1.1 fusion.61
  73.9 1.7 fusion.16
  75.8 0.3 mul.253
  76.1 0.2 copy.80
  76.3 1.6 copy.65
  77.9 76.9 %all-gather.5.cloned.1.call-done = bf16[1024,2688]{0,1:T(8,128)(2,1)} async-done(((bf16[1024,336]{0,1:T(8,128)(2,1)}), bf16[1024,2688]{0,1:T(8,128)(2,1)}) %all-gather.5.cloned.1.call-update) | async-done | bytes 5505040 | tf_op jit(solution)/shard_map/all_gather | solution.py:152
  154.8 5.9 %convolution_convert_fusion.2 = bf16[256,2688]{1,0:T(8,128)(2,1)} fusion(bf16[1024,2688]{0,1:T(8,128)(2,1)} %all-gather.5.cloned.1.call-done, f32[256,1024]{1,0:T(8,128)S(1)} %bitcast.145, f32[256,1024]{1,0:T(8,128)S(1)} %copy.65, bf16[256,1024]{1,0:T(8,128)(2,1)} %param.17, f32[1024]{0:T(1024)S(1)} %copy-done.13, f32[1024]{0:T(1024)S(1)} %mul.243, ...), kind=kOutput, calls=%fused_computation.16 | convolution fusion | flops 1413120000 | bytes 10035200 | tf_op jit(solution)/shard_map/dot_general | solution.py:155
  161.1 0.9 reduce-window.16
  162.0 0.2 slice_reduce_fusion
  162.8 23.2 %reduce-scatter.2.cloned.1.call-done = bf16[64,2688]{1,0:T(8,128)(2,1)} async-done(((bf16[256,2688]{1,0:T(8,128)(2,1)}), bf16[64,2688]{1,0:T(8,128)(2,1)}) %reduce-scatter.2.cloned.1.call-update) | async-done | bytes 344080 | tf_op jit(solution)/shard_map/reduce_scatter | solution.py:154
  186.0 1.2 multiply_reduce_fusion.1
  187.2 1.1 multiply_convert_fusion.2
  188.4 0.9 convolution_convert_fusion.1
  189.3 67.3 %all_to_all.10 = bf16[32,16,2688]{2,1,0:T(8,128)(2,1)S(1)} all-to-all(bf16[32,16,2688]{2,1,0:T(8,128)(2,1)S(1)} %bitcast.138), channel_id=1, replica_groups=mesh['grp'=1,'seq'=8,'head'=4] {'seq','head'}, dimensions={0} | all-to-all | bytes 5505024 | tf_op jit(solution)/shard_map/all_to_all | solution.py:192
  256.6 5.0 %collective-permute-done = bf16[32,16,2688]{2,1,0:T(8,128)(2,1)S(1)} collective-permute-done((bf16[32,16,2688]{2,1,0:T(8,128)(2,1)S(1)}, bf16[32,16,2688]{2,1,0:T(8,128)(2,1)S(1)}, u32[]{:S(2)}, u32[]{:S(2)}) %collective-permute-start) | collective-permute-done | bytes 2752544 | tf_op jit(solution)/shard_map/ppermute | solution.py:38
  261.7 2.8 pad_maximum_fusion
  264.5 18.9 %convolution_convert_fusion = bf16[1024,2688]{1,0:T(8,128)(2,1)} fusion(bf16[1,928,2688]{2,1,0:T(8,128)(2,1)} %param.31, bf16[1024,2688]{1,0:T(8,128)(2,1)} %bitcast.137, bf16[1,2688,928]{1,2,0:T(8,128)(2,1)} %param.30), kind=kOutput, calls=%fused_computation.4 | convolution fusion | flops 10222927872 | bytes 20987904 | tf_op jit(solution)/shard_map/dot_general | solution.py:47
  283.4 2.1 slice.35
  285.7 5.0 %collective-permute-done.1 = bf16[32,16,2688]{2,1,0:T(8,128)(2,1)S(1)} collective-permute-done((bf16[32,16,2688]{2,1,0:T(8,128)(2,1)S(1)}, bf16[32,16,2688]{2,1,0:T(8,128)(2,1)S(1)}, u32[]{:S(2)}, u32[]{:S(2)}) %collective-permute-start.1) | collective-permute-done | bytes 2752544 | tf_op jit(solution)/shard_map/ppermute | solution.py:38
  290.7 2.2 add_convert_fusion
  292.9 3.6 all-to-all-start.1
  297.1 62.4 %all-to-all-done.1 = bf16[32,16,2688]{2,1,0:T(8,128)(2,1)S(1)} async-done(((bf16[32,16,2688]{2,1,0:T(8,128)(2,1)}), bf16[32,16,2688]{2,1,0:T(8,128)(2,1)S(1)}, u32[]{:S(2)}, u32[]{:S(2)}) %all-to-all-start.1) | async-done | bytes 2752544 | tf_op jit(solution)/shard_map/all_to_all | solution.py:200
  359.5 3.4 gather_fusion
  362.9 4.6 %reshape.258 = f32[64,6,2688]{2,1,0:T(8,128)} reshape(bf16[384,2688]{1,0:T(8,128)(2,1)} %gather_fusion) | data formatting | bytes 6193152 | tf_op jit(solution)/shard_map/convert_element_type | solution.py:207
  367.5 4.6 %multiply_reduce_fusion = f32[64,2688]{1,0:T(8,128)S(1)} fusion(f32[64,6,2688]{2,1,0:T(8,128)} %reshape.258, f32[64,6]{1,0:T(8,128)S(1)} %copy.68), kind=kLoop, calls=%fused_computation.6 | loop fusion | flops 1892352 | bytes 4818432 | tf_op jit(solution)/shard_map/reduce_sum | solution.py:207
  372.1 0.8 add_convert_fusion.1
  (83 shorter events, 3.3 us)
Async XLA Ops:
  6.5 4.7 %copy-start = (bf16[256,256]{1,0:T(8,128)(2,1)S(1)}, bf16[256,256]{1,0:T(8,128)(2,1)}, u32[]{:S(2)}) copy-start(bf16[256,256]{1,0:T(8,128)(2,1)} %param.19) | copy-start | bytes 393220
  6.5 29.9 %copy-start.9 = (f32[256,16]{0,1:T(8,128)S(1)}, f32[256,16]{0,1:T(8,128)}, u32[]{:S(2)}) copy-start(f32[256,16]{0,1:T(8,128)} %param.21) | copy-start | bytes 49156
  6.5 29.1 %copy-start.6 = (bf16[256,1024]{1,0:T(8,128)(2,1)S(1)}, bf16[256,1024]{1,0:T(8,128)(2,1)}, u32[]{:S(2)}) copy-start(bf16[256,1024]{1,0:T(8,128)(2,1)} %param.18) | copy-start | bytes 1572868
  6.5 29.3 %copy-start.14 = (f32[16]{0:T(128)S(1)}, f32[16]{0:T(128)}, u32[]{:S(2)}) copy-start(f32[16]{0:T(128)} %param.23) | copy-start | bytes 196
  6.5 29.6 %copy-start.8 = (bf16[256,256]{1,0:T(8,128)(2,1)S(1)}, bf16[256,256]{1,0:T(8,128)(2,1)}, u32[]{:S(2)}) copy-start(bf16[256,256]{1,0:T(8,128)(2,1)} %param.20) | copy-start | bytes 393220
  6.5 58.1 %all-gather.7.cloned.1.call-start = ((), (), s32[]{:S(2)}) async-start(), calls=%async_computation.5 | async-start | bytes 2359296 | tf_op jit(solution)/shard_map/all_gather | solution.py:21
  12.5 142.3 %all-gather.5.cloned.1.call-start = ((), (), s32[]{:S(2)}) async-start(), calls=%async_computation.3 | async-start | bytes 6193152 | tf_op jit(solution)/shard_map/all_gather | solution.py:152
  13.3 172.8 %reduce-scatter.2.cloned.1.call-start = ((), (), s32[]{:S(2)}) async-start(), calls=%async_computation.4 | async-start | bytes 1720320 | tf_op jit(solution)/shard_map/reduce_scatter | solution.py:154
  75.6 79.2 %copy-start.7 = (bf16[256,1024]{1,0:T(8,128)(2,1)S(1)}, bf16[256,1024]{1,0:T(8,128)(2,1)}, u32[]{:S(2)}) copy-start(bf16[256,1024]{1,0:T(8,128)(2,1)} %param.18) | copy-start | bytes 1572868
  75.6 79.2 %copy-start.13 = (f32[1024]{0:T(1024)S(1)}, f32[1024]{0:T(1024)}, u32[]{:S(2)}) copy-start(f32[1024]{0:T(1024)} %param.24) | copy-start | bytes 12292
  154.8 6.0 %copy-start.11 = (s32[64,6]{0,1:T(8,128)S(1)}, s32[64,6]{0,1:T(8,128)}, u32[]{:S(2)}) copy-start(s32[64,6]{0,1:T(8,128)} %param.29) | copy-start | bytes 4612
  154.8 31.2 %copy-start.3 = (bf16[64,2688]{1,0:T(8,128)(2,1)S(1)}, bf16[64,2688]{1,0:T(8,128)(2,1)}, u32[]{:S(2)}) copy-start(bf16[64,2688]{1,0:T(8,128)(2,1)} %param.26) | copy-start | bytes 1032196
  154.8 32.4 %copy-start.12 = (f32[2688]{0:T(1024)S(1)}, f32[2688]{0:T(1024)}, u32[]{:S(2)}) copy-start(f32[2688]{0:T(1024)} %param.27) | copy-start | bytes 32260
  256.6 5.1 %collective-permute-start = (bf16[32,16,2688]{2,1,0:T(8,128)(2,1)S(1)}, bf16[32,16,2688]{2,1,0:T(8,128)(2,1)S(1)}, u32[]{:S(2)}, u32[]{:S(2)}) collective-permute-start(bf16[32,16,2688]{2,1,0:T(8,128)(2,1)S(1)} %all_to_all.10), channel_id=1, source_target_pairs={{0,1},{1,0},{2,3},{3,2},{4,5},{5,4},{6,7},{7,6},{8,9},{9,8},{10,11... | collective-permute-start | bytes 8257544 | tf_op jit(solution)/shard_map/ppermute | solution.py:38
  283.4 7.3 %copy-start.2 = (bf16[1024,2688]{1,0:T(8,128)(2,1)S(1)}, bf16[1024,2688]{1,0:T(8,128)(2,1)}, u32[]{:S(2)}) copy-start(bf16[1024,2688]{1,0:T(8,128)(2,1)} %convolution_convert_fusion) | copy-start | bytes 16515076
  285.5 5.2 %collective-permute-start.1 = (bf16[32,16,2688]{2,1,0:T(8,128)(2,1)S(1)}, bf16[32,16,2688]{2,1,0:T(8,128)(2,1)S(1)}, u32[]{:S(2)}, u32[]{:S(2)}) collective-permute-start(bf16[32,16,2688]{2,1,0:T(8,128)(2,1)S(1)} %slice.35), channel_id=1, source_target_pairs={{0,1},{1,0},{2,3},{3,2},{4,5},{5,4},{6,7},{7,6},{8,9},{9,8},{10,11... | collective-permute-start | bytes 8257544 | tf_op jit(solution)/shard_map/ppermute | solution.py:38
  292.9 3.8 copy-start.10
  292.9 66.6 %all-to-all-start.1 = ((bf16[32,16,2688]{2,1,0:T(8,128)(2,1)}), bf16[32,16,2688]{2,1,0:T(8,128)(2,1)S(1)}, u32[]{:S(2)}, u32[]{:S(2)}) async-start(bf16[32,16,2688]{2,1,0:T(8,128)(2,1)} %add_convert_fusion), calls=%async_computation.2 | async-start | bytes 5505024 | tf_op jit(solution)/shard_map/all_to_all | solution.py:200
  362.9 10.0 %copy-start.1 = (bf16[256,256]{1,0:T(8,128)(2,1)S(1)}, bf16[256,256]{1,0:T(8,128)(2,1)}, u32[]{:S(2)}) copy-start(bf16[256,256]{1,0:T(8,128)(2,1)} %param.19) | copy-start | bytes 393220
  367.5 4.6 %copy-start.4 = (bf16[64,2688]{1,0:T(8,128)(2,1)S(1)}, bf16[64,2688]{1,0:T(8,128)(2,1)}, u32[]{:S(2)}) copy-start(bf16[64,2688]{1,0:T(8,128)(2,1)} %param.26) | copy-start | bytes 1032196
  367.5 4.6 %copy-start.5 = (bf16[64,2688]{1,0:T(8,128)(2,1)S(1)}, bf16[64,2688]{1,0:T(8,128)(2,1)}, u32[]{:S(2)}) copy-start(bf16[64,2688]{1,0:T(8,128)(2,1)} %reduce-scatter.2.cloned.1.call-done) | copy-start | bytes 1032196
Sparse Core Ops, SparseCore 0:
  12.6 51.9 all-gather.6
  66.8 87.9 all-gather.4
  160.9 25.1 reduce-scatter.1
where the time goes:
time: 380 us; the launch traced here: 379 us
  waiting for transfers between devices  200 us (53%)
  blocking collectives  89.4 us (24%)
  matrix products  29.6 us (8%)
  other arithmetic  27.3 us (7%)
  local copies, waits for them, and re-layouts  15.9 us (4%)
  between operations  13.5 us (4%)
  starting transfers between devices  3.95 us (1%)
    all_gather x1, waiting for transfers between devices, per_device(): weight_full = lax.all_gather(out_weight, 'seq', axis=1, tiled=True)  76.9 us
    all_to_all x1, blocking collectives, per_device(): lax.all_to_all(halves, ('seq', 'head'), split_axis=0, concat_axis=0, tile...  67.3 us
    all_to_all x1, waiting for transfers between devices, per_device(): lax.all_to_all(summed, ('seq', 'head'), split_axis=0, concat_axis=0, tile...  62.4 us
    all_gather x1, waiting for transfers between devices, entering(): lax.all_gather(part.astype(kind), axis)  26.3 us
    reduce_scatter x1, waiting for transfers between devices, per_device(): lax.psum_scatter(jnp.dot(normed, weight_full, preferred_element_type=jnp....  23.2 us
    all_gather x1, blocking collectives, entering(): lax.all_gather(part.astype(kind), axis)  22.2 us
    dot_general x1, matrix products, expert_half(): jnp.dot(activation, down_weight[0], preferred_element_type=jnp.float32)  18.9 us
    ppermute x2, waiting for transfers between devices, partner(): lax.ppermute(x, axis, [(i, i ^ 1 << stride) for i in range(lax.axis_size(...  9.99 us
  transfers between devices with their start and end apart: 6, of which 6 were waited for; matrix products, arithmetic and copies ran while one was open for 5% of the time, Pallas kernels for 0%

commit v1 on v0

--- a/solution.py
+++ b/solution.py
@@ -15,23 +15,87 @@
 ROUTE_SCALE = 2.5
 
 
-def entering(x, axis, combine, identity):
-    size, mine = (lax.axis_size(axis), lax.axis_index(axis))
-    everything = jax.tree.map(
-        lambda part, kind: lax.all_gather(part.astype(kind), axis), x, (jnp.bfloat16, jnp.bfloat16)
-    )
-    start = jax.tree.map(
-        lambda part, zero: jnp.broadcast_to(jnp.asarray(zero, part.dtype), part.shape), x, identity
-    )
-
-    def turn(k, before):
-        reached = k < mine
-        new = combine(
-            before, jax.tree.map(lambda part, own: part[k].astype(own.dtype), everything, x)
-        )
-        return jax.tree.map(lambda a, b: jnp.where(reached, a, b), new, before)
-
-    return lax.fori_loop(0, size, turn, start)
+def shift(x, axis, step):
+    size = lax.axis_size(axis)
+    pairs = [(i, i + step) for i in range(size) if 0 <= i + step < size]
+    return lax.ppermute(x, axis, pairs)
+
+
+def entering(decay, state):
+    count = lax.axis_size("seq") // 2
+    odd = lax.axis_index("seq") % 2 == 1
+    heads, rows, width = state.shape
+
+    def pack(decay, state):
+        tail = jnp.broadcast_to(decay[:, None, None], (heads, 8, width))
+        return jnp.concatenate([state, tail], axis=1).astype(jnp.bfloat16)
+
+    def unpack(packed):
+        wide = packed.astype(jnp.float32)
+        return wide[:, rows, 0], wide[:, :rows]
+
+    def combine(earlier, later):
+        return (earlier[0] * later[0], later[0][:, None, None] * earlier[1] + later[1])
+
+    mine = (decay, state)
+    other = unpack(partner(pack(*mine), "seq", 0))
+    first = jax.tree.map(lambda a, b: jnp.where(odd, a, b), other, mine)
+    second = jax.tree.map(lambda a, b: jnp.where(odd, a, b), mine, other)
+    before = jax.tree.map(lambda a: jnp.where(odd, a, jnp.zeros_like(a)), other)
+    before = (jnp.where(odd, before[0], 1.0), before[1])
+    pair = combine(first, second)
+    reach, scan = 1, unpack(shift(pack(*pair), "seq", 2))
+    while reach < count - 1:
+        scan = combine(unpack(shift(pack(*scan), "seq", 2 * reach)), scan)
+        reach *= 2
+    return combine(scan, before)[1]
+
+
+def gather_columns(block):
+    count = lax.axis_size("seq") // 2
+    place = lax.axis_index("seq") // 2
+    up, down = [block], [block]
+    for step in range(1, count):
+        up.append(shift(up[-1], "seq", 2))
+        down.append(shift(down[-1], "seq", -2))
+    slots = [block]
+    for step in range(1, count):
+        slots.append(jnp.where(place + step < count, down[step], up[count - step]))
+    return [(slot, partner(slot, "seq", 0)) for slot in slots]
+
+
+def project(normed, slots):
+    count = len(slots)
+    place, odd = lax.axis_index("seq") // 2, lax.axis_index("seq") % 2 == 1
+    parts = []
+    for pair in slots:
+        first, second = (
+            jnp.dot(normed, block, preferred_element_type=jnp.float32).astype(jnp.bfloat16)
+            for block in pair
+        )
+        parts.append(
+            jnp.concatenate(
+                [jnp.where(odd, second, first), jnp.where(odd, first, second)], axis=1
+            )
+        )
+    parts = jnp.stack(parts + parts[:-1])
+    parts = lax.dynamic_slice_in_dim(parts, (count - place) % count, count, axis=0)
+    return parts.transpose(1, 0, 2).reshape(normed.shape[0], -1)
+
+
+def sum_rows(x, axis):
+    size = lax.axis_size(axis)
+    bits = size.bit_length() - 1
+    width = x.shape[-1]
+    x = x.reshape((2,) * bits + (-1, width))
+    for bit in range(bits):
+        mine = lax.axis_index(axis) >> bit & 1
+        where = bits - 1 - bit
+        keep = lax.dynamic_index_in_dim(x, mine, where, keepdims=False)
+        give = lax.dynamic_index_in_dim(x, 1 - mine, where, keepdims=False)
+        got = partner(give.astype(jnp.bfloat16), axis, bit)
+        x = keep.astype(jnp.float32) + got.astype(jnp.float32)
+    return x
 
 
 def partner(x, axis, stride):
@@ -67,6 +131,7 @@
     up_weight,
     down_weight,
 ):
+    slots = gather_columns(out_weight)
     tokens_dev = ssm_values.shape[0]
     heads_dev = step_size.shape[1]
     per_group = HEADS // GROUPS
@@ -118,11 +183,7 @@
         summarize, (jnp.ones((heads_dev,), jnp.float32), zero_state), (totals_blk, fresh_all)
     )
 
-    def combine(earlier, later):
-        return (earlier[0] * later[0], later[0][:, None, None] * earlier[1] + later[1])
-
-    identity = (jnp.ones_like(device_decay), jnp.zeros_like(device_state))
-    prior_decay, incoming = entering((device_decay, device_state), "seq", combine, identity)
+    incoming = entering(device_decay, device_state)
 
     def emit_rows(carry_state, pieces):
         read_in, cumulative, block_total, fresh_state = pieces
@@ -149,14 +210,8 @@
     normed = (
         (gated * inv_rms).reshape(tokens_dev, heads_dev * HEAD_DIM) * norm_gain[None, :]
     ).astype(jnp.bfloat16)
-    weight_full = lax.all_gather(out_weight, "seq", axis=1, tiled=True)
     rows_own = tokens_dev // lax.axis_size("head")
-    mixed_out = lax.psum_scatter(
-        jnp.dot(normed, weight_full, preferred_element_type=jnp.float32).astype(jnp.bfloat16),
-        "head",
-        scatter_dimension=0,
-        tiled=True,
-    ).astype(jnp.float32)
+    mixed_out = sum_rows(project(normed, slots), "head")
     hidden = residual.astype(jnp.float32) + mixed_out
     inputs = (
         hidden

time: 380 us -> 337 us (0.89)
  waiting for transfers between devices: 200 us -> 143 us
  starting transfers between devices: 3.95 us -> 51.5 us
  blocking collectives: 89.4 us -> 69.3 us
  between operations: 13.5 us -> 0.76 us
  other arithmetic: 27.3 us -> 21.7 us
  local copies, waits for them, and re-layouts: 15.9 us -> 20.1 us
    all_gather x2 -> x0, waiting for transfers between devices: 103 us -> none  [the longest x1 76.9 us: per_device(): weight_full = lax.all_gather(out_weight, 'seq', axis=1, tiled=True)]
    ppermute x2 -> x9, waiting for transfers between devices: 9.99 us -> 51.8 us  [partner(): lax.ppermute(x, axis, [(i, i ^ 1 << stride) for i in range(lax.axis_size(...]
    ppermute x0 -> x9, starting transfers between devices: none -> 35.7 us  [shift(): return lax.ppermute(x, axis, pairs)]
    ppermute x0 -> x9, waiting for transfers between devices: none -> 29.9 us  [shift(): return lax.ppermute(x, axis, pairs)]
    reduce_scatter x1 -> x0, waiting for transfers between devices: 23.2 us -> none  [per_device(): lax.psum_scatter(jnp.dot(normed, weight_full, preferred_element_type=jnp....]
    all_gather x1 -> x0, blocking collectives: 22.2 us -> none  [entering(): lax.all_gather(part.astype(kind), axis)]
    ppermute x2 -> x9, starting transfers between devices: 0.27 us -> 12.3 us  [partner(): lax.ppermute(x, axis, [(i, i ^ 1 << stride) for i in range(lax.axis_size(...]
    select_n x8 -> x4, other arithmetic: 8.78 us -> 2.66 us  [the longest x3 2.46 us: gather_columns(): slots.append(jnp.where(place + step < count, down[step], up[count - step]))]
  transfers between devices with their start and end apart: 6 -> 19, of which waited for: 6 -> 12; matrix products, arithmetic and copies ran while one was open for 5% -> 6% of each run, Pallas kernels for 0% -> 0%
where the time goes in v1:
time: 337 us; the launch traced here: 336 us
  waiting for transfers between devices  143 us (42%)
  blocking collectives  69.3 us (21%)
  starting transfers between devices  51.5 us (15%)
  matrix products  29.5 us (9%)
  other arithmetic  21.7 us (6%)
  local copies, waits for them, and re-layouts  20.1 us (6%)
    all_to_all x1, blocking collectives, per_device(): lax.all_to_all(halves, ('seq', 'head'), split_axis=0, concat_axis=0, tile...  69.3 us
    all_to_all x1, waiting for transfers between devices, per_device(): lax.all_to_all(summed, ('seq', 'head'), split_axis=0, concat_axis=0, tile...  61.3 us
    ppermute x9, waiting for transfers between devices, partner(): lax.ppermute(x, axis, [(i, i ^ 1 << stride) for i in range(lax.axis_size(...  51.8 us
    ppermute x9, starting transfers between devices, shift(): return lax.ppermute(x, axis, pairs)  35.7 us
    ppermute x9, waiting for transfers between devices, shift(): return lax.ppermute(x, axis, pairs)  29.9 us
    dot_general x1, matrix products, expert_half(): jnp.dot(activation, down_weight[0], preferred_element_type=jnp.float32)  18.9 us
    ppermute x9, starting transfers between devices, partner(): lax.ppermute(x, axis, [(i, i ^ 1 << stride) for i in range(lax.axis_size(...  12.3 us
  transfers between devices with their start and end apart: 19, of which 12 were waited for; matrix products, arithmetic and copies ran while one was open for 6% of the time, Pallas kernels for 0%

profile of v1, /device:TPU:0, one launch (start us, length us, event | category | flops | bytes accessed | tf_op | source)
XLA Modules:
  0.0 335.8 jit_solution(14382721103453533076)
XLA Ops:
  3.4 1.2 copy.72
  5.3 3.0 collective-permute-start
  8.3 7.0 %collective-permute-done = bf16[16,72,128]{2,1,0:T(8,128)(2,1)S(1)} collective-permute-done((bf16[16,72,128]{2,1,0:T(8,128)(2,1)S(1)}, bf16[16,72,128]{2,1,0:T(8,128)(2,1)S(1)}, u32[]{:S(2)}, u32[]{:S(2)}) %collective-permute-start) | collective-permute-done | bytes 294944 | tf_op jit(solution)/shard_map/ppermute | solution.py:102
  16.1 3.7 %collective-permute-start.1 = (bf16[16,72,128]{2,1,0:T(8,128)(2,1)S(1)}, bf16[16,72,128]{2,1,0:T(8,128)(2,1)S(1)}, u32[]{:S(2)}, u32[]{:S(2)}) collective-permute-start(bf16[16,72,128]{2,1,0:T(8,128)(2,1)S(1)} %pad_maximum_fusion.2), channel_id=1, source_target_pairs={{0,8},{4,12},{8,16},{12,20},{16,24},{20,28},{1,9},{5,13},{9,17},{1... | collective-permute-start | bytes 884744 | tf_op jit(solution)/shard_map/ppermute | solution.py:21
  19.8 1.6 collective-permute-start.4
  21.4 1.3 collective-permute-start.5
  22.7 5.4 %collective-permute-start.6 = (bf16[1024,336]{0,1:T(8,128)(2,1)}, bf16[1024,336]{0,1:T(8,128)(2,1)}, u32[]{:S(2)}, u32[]{:S(2)}) collective-permute-start(bf16[1024,336]{0,1:T(8,128)(2,1)} %param.23), channel_id=1, source_target_pairs={{0,8},{4,12},{8,16},{12,20},{16,24},{20,28},{1,9},{5,13},{9,17},{1... | collective-permute-start | bytes 2064392 | tf_op jit(solution)/shard_map/ppermute | solution.py:21
  28.1 1.2 copy.78
  30.2 2.7 collective-permute-start.2
  32.9 1.2 fusion.5
  34.1 12.6 %collective-permute-done.2 = bf16[16,72,128]{2,1,0:T(8,128)(2,1)S(1)} collective-permute-done((bf16[16,72,128]{2,1,0:T(8,128)(2,1)S(1)}, bf16[16,72,128]{2,1,0:T(8,128)(2,1)S(1)}, u32[]{:S(2)}, u32[]{:S(2)}) %collective-permute-start.2) | collective-permute-done | bytes 294944 | tf_op jit(solution)/shard_map/ppermute | solution.py:21
  47.3 5.5 %collective-permute-start.3 = (bf16[16,72,128]{2,1,0:T(8,128)(2,1)S(1)}, bf16[16,72,128]{2,1,0:T(8,128)(2,1)S(1)}, u32[]{:S(2)}, u32[]{:S(2)}) collective-permute-start(bf16[16,72,128]{2,1,0:T(8,128)(2,1)S(1)} %pad_maximum_fusion.4), channel_id=1, source_target_pairs={{0,16},{4,20},{8,24},{12,28},{1,17},{5,21},{9,25},{13,29},{2,18},{... | collective-permute-start | bytes 884744 | tf_op jit(solution)/shard_map/ppermute | solution.py:21
  53.6 5.2 %collective-permute-start.7 = (bf16[1024,336]{0,1:T(8,128)(2,1)}, bf16[1024,336]{0,1:T(8,128)(2,1)}, u32[]{:S(2)}, u32[]{:S(2)}) collective-permute-start(bf16[1024,336]{0,1:T(8,128)(2,1)} %collective-permute-done.6), channel_id=1, source_target_pairs={{0,8},{4,12},{8,16},{12,20},{16,24},{20,28},{1,9},{5,13},{9,17},{1... | collective-permute-start | bytes 2064392 | tf_op jit(solution)/shard_map/ppermute | solution.py:21
  58.8 1.3 collective-permute-start.10
  60.3 1.8 fusion.14
  62.8 1.6 copy.77
  64.9 7.0 %collective-permute-done.7 = bf16[1024,336]{0,1:T(8,128)(2,1)} collective-permute-done((bf16[1024,336]{0,1:T(8,128)(2,1)}, bf16[1024,336]{0,1:T(8,128)(2,1)}, u32[]{:S(2)}, u32[]{:S(2)}) %collective-permute-start.7) | collective-permute-done | bytes 688160 | tf_op jit(solution)/shard_map/ppermute | solution.py:21
  71.9 9.1 %collective-permute-start.8 = (bf16[1024,336]{0,1:T(8,128)(2,1)}, bf16[1024,336]{0,1:T(8,128)(2,1)S(1)}, u32[]{:S(2)}, u32[]{:S(2)}) collective-permute-start(bf16[1024,336]{0,1:T(8,128)(2,1)} %collective-permute-done.7), channel_id=1, source_target_pairs={{0,8},{4,12},{8,16},{12,20},{16,24},{20,28},{1,9},{5,13},{9,17},{1... | collective-permute-start | bytes 2064392 | tf_op jit(solution)/shard_map/ppermute | solution.py:21
  81.0 1.5 convolution_convert_fusion.8
  82.5 1.5 collective-permute-start.12
  84.0 1.2 broadcast_select_fusion.1
  85.2 1.5 collective-permute-start.11
  86.7 1.5 broadcast_select_fusion.10
  88.2 7.2 %collective-permute-done.8 = bf16[1024,336]{0,1:T(8,128)(2,1)S(1)} collective-permute-done((bf16[1024,336]{0,1:T(8,128)(2,1)}, bf16[1024,336]{0,1:T(8,128)(2,1)S(1)}, u32[]{:S(2)}, u32[]{:S(2)}) %collective-permute-start.8) | collective-permute-done | bytes 688160 | tf_op jit(solution)/shard_map/ppermute | solution.py:21
  95.5 1.2 broadcast_select_fusion.2
  96.6 2.1 collective-permute-start.9
  98.8 2.9 collective-permute-done.12
  101.8 2.1 collective-permute-start.13
  104.8 13.6 %collective-permute-done.9 = bf16[1024,336]{0,1:T(8,128)(2,1)S(1)} collective-permute-done((bf16[1024,336]{0,1:T(8,128)(2,1)S(1)}, bf16[1024,336]{0,1:T(8,128)(2,1)S(1)}, u32[]{:S(2)}, u32[]{:S(2)}) %collective-permute-start.9) | collective-permute-done | bytes 688160 | tf_op jit(solution)/shard_map/ppermute | solution.py:102
  119.2 12.3 %collective-permute-done.13 = bf16[1024,336]{0,1:T(8,128)(2,1)S(1)} collective-permute-done((bf16[1024,336]{0,1:T(8,128)(2,1)S(1)}, bf16[1024,336]{0,1:T(8,128)(2,1)S(1)}, u32[]{:S(2)}, u32[]{:S(2)}) %collective-permute-start.13) | collective-permute-done | bytes 688160 | tf_op jit(solution)/shard_map/ppermute | solution.py:102
  132.6 1.3 copy.80
  133.8 1.2 reshape_reshape.3
  137.4 1.2 convert_add_fusion
  138.7 1.5 collective-permute-start.15
  140.5 8.4 %collective-permute-done.15 = bf16[64,2688]{1,0:T(8,128)(2,1)S(1)} collective-permute-done((bf16[64,2688]{1,0:T(8,128)(2,1)S(1)}, bf16[64,2688]{1,0:T(8,128)(2,1)S(1)}, u32[]{:S(2)}, u32[]{:S(2)}) %collective-permute-start.15) | collective-permute-done | bytes 344096 | tf_op jit(solution)/shard_map/ppermute | solution.py:102
  150.1 69.3 %all_to_all.10 = bf16[32,16,2688]{2,1,0:T(8,128)(2,1)S(1)} all-to-all(bf16[32,16,2688]{2,1,0:T(8,128)(2,1)S(1)} %bitcast.174), channel_id=1, replica_groups=mesh['grp'=1,'seq'=8,'head'=4] {'seq','head'}, dimensions={0} | all-to-all | bytes 5505024 | tf_op jit(solution)/shard_map/all_to_all | solution.py:247
  219.6 5.0 %collective-permute-done.16 = bf16[32,16,2688]{2,1,0:T(8,128)(2,1)S(1)} collective-permute-done((bf16[32,16,2688]{2,1,0:T(8,128)(2,1)S(1)}, bf16[32,16,2688]{2,1,0:T(8,128)(2,1)S(1)}, u32[]{:S(2)}, u32[]{:S(2)}) %collective-permute-start.16) | collective-permute-done | bytes 2752544 | tf_op jit(solution)/shard_map/ppermute | solution.py:102
  224.6 2.8 pad_maximum_fusion
  227.4 18.9 %convolution_convert_fusion = bf16[1024,2688]{1,0:T(8,128)(2,1)} fusion(bf16[1,928,2688]{2,1,0:T(8,128)(2,1)} %param.29, bf16[1024,2688]{1,0:T(8,128)(2,1)} %bitcast.173, bf16[1,2688,928]{1,2,0:T(8,128)(2,1)} %param.28), kind=kOutput, calls=%fused_computation.1 | convolution fusion | flops 10222927872 | bytes 20987904 | tf_op jit(solution)/shard_map/dot_general | solution.py:111
  246.3 2.1 slice.74
  248.7 4.9 %collective-permute-done.17 = bf16[32,16,2688]{2,1,0:T(8,128)(2,1)S(1)} collective-permute-done((bf16[32,16,2688]{2,1,0:T(8,128)(2,1)S(1)}, bf16[32,16,2688]{2,1,0:T(8,128)(2,1)S(1)}, u32[]{:S(2)}, u32[]{:S(2)}) %collective-permute-start.17) | collective-permute-done | bytes 2752544 | tf_op jit(solution)/shard_map/ppermute | solution.py:102
  253.6 2.2 add_convert_fusion
  255.8 3.6 %all-to-all-start.1 = ((bf16[32,16,2688]{2,1,0:T(8,128)(2,1)}), bf16[32,16,2688]{2,1,0:T(8,128)(2,1)S(1)}, u32[]{:S(2)}, u32[]{:S(2)}) async-start(bf16[32,16,2688]{2,1,0:T(8,128)(2,1)} %add_convert_fusion), calls=%async_computation.1 | async-start | bytes 5505024 | tf_op jit(solution)/shard_map/all_to_all | solution.py:255
  259.6 1.4 fusion.51
  261.1 61.3 %all-to-all-done.1 = bf16[32,16,2688]{2,1,0:T(8,128)(2,1)S(1)} async-done(((bf16[32,16,2688]{2,1,0:T(8,128)(2,1)}), bf16[32,16,2688]{2,1,0:T(8,128)(2,1)S(1)}, u32[]{:S(2)}, u32[]{:S(2)}) %all-to-all-start.1) | async-done | bytes 2752544 | tf_op jit(solution)/shard_map/all_to_all | solution.py:255
  322.4 3.4 %gather_fusion = bf16[384,2688]{1,0:T(8,128)(2,1)} fusion(bf16[512,2688]{1,0:T(8,128)(2,1)S(1)} %bitcast.170, s32[1024]{0:T(1024)S(1)} %pad_clamp_fusion), kind=kCustom, calls=%fused_computation | custom fusion | bytes 4130304 | tf_op jit(solution)/shard_map/gather | solution.py:259
  325.8 4.6 %reshape.257 = f32[64,6,2688]{2,1,0:T(8,128)} reshape(bf16[384,2688]{1,0:T(8,128)(2,1)} %gather_fusion) | data formatting | bytes 6193152 | tf_op jit(solution)/shard_map/convert_element_type | solution.py:262
  330.4 4.6 %multiply_reduce_fusion = f32[64,2688]{1,0:T(8,128)S(1)} fusion(f32[64,6,2688]{2,1,0:T(8,128)} %reshape.257, f32[64,6]{1,0:T(8,128)S(1)} %copy.81), kind=kLoop, calls=%fused_computation.3 | loop fusion | flops 1892352 | bytes 4818432 | tf_op jit(solution)/shard_map/reduce_sum | solution.py:262
  (130 shorter events, 16.2 us)
Async XLA Ops:
  0.0 4.6 %copy-start = (bf16[256,256]{1,0:T(8,128)(2,1)S(1)}, bf16[256,256]{1,0:T(8,128)(2,1)}, u32[]{:S(2)}) copy-start(bf16[256,256]{1,0:T(8,128)(2,1)} %param.17) | copy-start | bytes 393220
  4.8 23.3 %copy-start.5 = (bf16[256,1024]{1,0:T(8,128)(2,1)S(1)}, bf16[256,1024]{1,0:T(8,128)(2,1)}, u32[]{:S(2)}) copy-start(bf16[256,1024]{1,0:T(8,128)(2,1)} %param.16) | copy-start | bytes 1572868
  5.2 24.2 %copy-start.15 = (f32[16]{0:T(128)S(1)}, f32[16]{0:T(128)}, u32[]{:S(2)}) copy-start(f32[16]{0:T(128)} %param.21) | copy-start | bytes 196
  5.2 24.4 %copy-start.8 = (bf16[256,256]{1,0:T(8,128)(2,1)S(1)}, bf16[256,256]{1,0:T(8,128)(2,1)}, u32[]{:S(2)}) copy-start(bf16[256,256]{1,0:T(8,128)(2,1)} %param.18) | copy-start | bytes 393220
  5.3 10.0 %collective-permute-start = (bf16[16,72,128]{2,1,0:T(8,128)(2,1)S(1)}, bf16[16,72,128]{2,1,0:T(8,128)(2,1)S(1)}, u32[]{:S(2)}, u32[]{:S(2)}) collective-permute-start(bf16[16,72,128]{2,1,0:T(8,128)(2,1)S(1)} %pad_maximum_fusion.1), channel_id=1, source_target_pairs={{0,4},{4,0},{8,12},{12,8},{16,20},{20,16},{24,28},{28,24},{1,5},{5... | collective-permute-start | bytes 884744 | tf_op jit(solution)/shard_map/ppermute | solution.py:102
  16.0 16.9 %copy-start.10 = (f32[256,16]{0,1:T(8,128)S(1)}, f32[256,16]{0,1:T(8,128)}, u32[]{:S(2)}) copy-start(f32[256,16]{0,1:T(8,128)} %param.19) | copy-start | bytes 49156
  16.1 13.7 %collective-permute-start.1 = (bf16[16,72,128]{2,1,0:T(8,128)(2,1)S(1)}, bf16[16,72,128]{2,1,0:T(8,128)(2,1)S(1)}, u32[]{:S(2)}, u32[]{:S(2)}) collective-permute-start(bf16[16,72,128]{2,1,0:T(8,128)(2,1)S(1)} %pad_maximum_fusion.2), channel_id=1, source_target_pairs={{0,8},{4,12},{8,16},{12,20},{16,24},{20,28},{1,9},{5,13},{9,17},{1... | collective-permute-start | bytes 884744 | tf_op jit(solution)/shard_map/ppermute | solution.py:21
  19.8 66.9 %collective-permute-start.4 = (bf16[1024,336]{0,1:T(8,128)(2,1)}, bf16[1024,336]{0,1:T(8,128)(2,1)}, u32[]{:S(2)}, u32[]{:S(2)}) collective-permute-start(bf16[1024,336]{0,1:T(8,128)(2,1)} %param.23), channel_id=1, source_target_pairs={{0,4},{4,0},{8,12},{12,8},{16,20},{20,16},{24,28},{28,24},{1,5},{5... | collective-permute-start | bytes 2064392 | tf_op jit(solution)/shard_map/ppermute | solution.py:102
  21.4 37.4 %collective-permute-start.5 = (bf16[1024,336]{0,1:T(8,128)(2,1)}, bf16[1024,336]{0,1:T(8,128)(2,1)}, u32[]{:S(2)}, u32[]{:S(2)}) collective-permute-start(bf16[1024,336]{0,1:T(8,128)(2,1)} %param.23), channel_id=1, source_target_pairs={{8,0},{12,4},{16,8},{20,12},{24,16},{28,20},{9,1},{13,5},{17,9},{2... | collective-permute-start | bytes 2064392 | tf_op jit(solution)/shard_map/ppermute | solution.py:21
  22.7 30.9 %collective-permute-start.6 = (bf16[1024,336]{0,1:T(8,128)(2,1)}, bf16[1024,336]{0,1:T(8,128)(2,1)}, u32[]{:S(2)}, u32[]{:S(2)}) collective-permute-start(bf16[1024,336]{0,1:T(8,128)(2,1)} %param.23), channel_id=1, source_target_pairs={{0,8},{4,12},{8,16},{12,20},{16,24},{20,28},{1,9},{5,13},{9,17},{1... | collective-permute-start | bytes 2064392 | tf_op jit(solution)/shard_map/ppermute | solution.py:21
  30.2 16.5 %collective-permute-start.2 = (bf16[16,72,128]{2,1,0:T(8,128)(2,1)S(1)}, bf16[16,72,128]{2,1,0:T(8,128)(2,1)S(1)}, u32[]{:S(2)}, u32[]{:S(2)}) collective-permute-start(bf16[16,72,128]{2,1,0:T(8,128)(2,1)S(1)} %pad_maximum_fusion.3), channel_id=1, source_target_pairs={{0,8},{4,12},{8,16},{12,20},{16,24},{20,28},{1,9},{5,13},{9,17},{1... | collective-permute-start | bytes 884744 | tf_op jit(solution)/shard_map/ppermute | solution.py:21
  47.1 13.1 %copy-start.7 = (f32[256,1024]{0,1:T(8,128)S(1)}, f32[256,1024]{0,1:T(8,128)}, u32[]{:S(2)}) copy-start(f32[256,1024]{0,1:T(8,128)} %copy.78) | copy-start | bytes 3145732
  47.3 12.8 %collective-permute-start.3 = (bf16[16,72,128]{2,1,0:T(8,128)(2,1)S(1)}, bf16[16,72,128]{2,1,0:T(8,128)(2,1)S(1)}, u32[]{:S(2)}, u32[]{:S(2)}) collective-permute-start(bf16[16,72,128]{2,1,0:T(8,128)(2,1)S(1)} %pad_maximum_fusion.4), channel_id=1, source_target_pairs={{0,16},{4,20},{8,24},{12,28},{1,17},{5,21},{9,25},{13,29},{2,18},{... | collective-permute-start | bytes 884744 | tf_op jit(solution)/shard_map/ppermute | solution.py:21
  53.6 18.3 %collective-permute-start.7 = (bf16[1024,336]{0,1:T(8,128)(2,1)}, bf16[1024,336]{0,1:T(8,128)(2,1)}, u32[]{:S(2)}, u32[]{:S(2)}) collective-permute-start(bf16[1024,336]{0,1:T(8,128)(2,1)} %collective-permute-done.6), channel_id=1, source_target_pairs={{0,8},{4,12},{8,16},{12,20},{16,24},{20,28},{1,9},{5,13},{9,17},{1... | collective-permute-start | bytes 2064392 | tf_op jit(solution)/shard_map/ppermute | solution.py:21
  58.8 23.7 %collective-permute-start.10 = (bf16[1024,336]{0,1:T(8,128)(2,1)}, bf16[1024,336]{0,1:T(8,128)(2,1)}, u32[]{:S(2)}, u32[]{:S(2)}) collective-permute-start(bf16[1024,336]{0,1:T(8,128)(2,1)} %collective-permute-done.5), channel_id=1, source_target_pairs={{8,0},{12,4},{16,8},{20,12},{24,16},{28,20},{9,1},{13,5},{17,9},{2... | collective-permute-start | bytes 2064392 | tf_op jit(solution)/shard_map/ppermute | solution.py:21
  62.1 2.3 copy-start.6
  62.1 2.3 copy-start.14
  71.9 23.6 %collective-permute-start.8 = (bf16[1024,336]{0,1:T(8,128)(2,1)}, bf16[1024,336]{0,1:T(8,128)(2,1)S(1)}, u32[]{:S(2)}, u32[]{:S(2)}) collective-permute-start(bf16[1024,336]{0,1:T(8,128)(2,1)} %collective-permute-done.7), channel_id=1, source_target_pairs={{0,8},{4,12},{8,16},{12,20},{16,24},{20,28},{1,9},{5,13},{9,17},{1... | collective-permute-start | bytes 2064392 | tf_op jit(solution)/shard_map/ppermute | solution.py:21
  82.5 19.2 %collective-permute-start.12 = (bf16[1024,336]{0,1:T(8,128)(2,1)}, bf16[1024,336]{0,1:T(8,128)(2,1)S(1)}, u32[]{:S(2)}, u32[]{:S(2)}) collective-permute-start(bf16[1024,336]{0,1:T(8,128)(2,1)} %collective-permute-done.10), channel_id=1, source_target_pairs={{8,0},{12,4},{16,8},{20,12},{24,16},{28,20},{9,1},{13,5},{17,9},{2... | collective-permute-start | bytes 2064392 | tf_op jit(solution)/shard_map/ppermute | solution.py:21
  85.2 18.8 %collective-permute-start.11 = (bf16[1024,336]{0,1:T(8,128)(2,1)S(1)}, bf16[1024,336]{0,1:T(8,128)(2,1)S(1)}, u32[]{:S(2)}, u32[]{:S(2)}) collective-permute-start(bf16[1024,336]{0,1:T(8,128)(2,1)S(1)} %broadcast_select_fusion.1), channel_id=1, source_target_pairs={{0,4},{4,0},{8,12},{12,8},{16,20},{20,16},{24,28},{28,24},{1,5},{5... | collective-permute-start | bytes 2064392 | tf_op jit(solution)/shard_map/ppermute | solution.py:102
  96.6 21.7 %collective-permute-start.9 = (bf16[1024,336]{0,1:T(8,128)(2,1)S(1)}, bf16[1024,336]{0,1:T(8,128)(2,1)S(1)}, u32[]{:S(2)}, u32[]{:S(2)}) collective-permute-start(bf16[1024,336]{0,1:T(8,128)(2,1)S(1)} %broadcast_select_fusion.2), channel_id=1, source_target_pairs={{0,4},{4,0},{8,12},{12,8},{16,20},{20,16},{24,28},{28,24},{1,5},{5... | collective-permute-start | bytes 2064392 | tf_op jit(solution)/shard_map/ppermute | solution.py:102
  101.8 29.6 %collective-permute-start.13 = (bf16[1024,336]{0,1:T(8,128)(2,1)S(1)}, bf16[1024,336]{0,1:T(8,128)(2,1)S(1)}, u32[]{:S(2)}, u32[]{:S(2)}) collective-permute-start(bf16[1024,336]{0,1:T(8,128)(2,1)S(1)} %broadcast_select_fusion), channel_id=1, source_target_pairs={{0,4},{4,0},{8,12},{12,8},{16,20},{20,16},{24,28},{28,24},{1,5},{5... | collective-permute-start | bytes 2064392 | tf_op jit(solution)/shard_map/ppermute | solution.py:102
  133.8 1.4 copy-start.13
  135.0 13.9 %copy-start.9 = (bf16[64,2688]{1,0:T(8,128)(2,1)S(1)}, bf16[64,2688]{1,0:T(8,128)(2,1)}, u32[]{:S(2)}) copy-start(bf16[64,2688]{1,0:T(8,128)(2,1)} %param.24) | copy-start | bytes 1032196
  135.1 2.3 collective-permute-start.14
  137.0 12.2 %copy-start.12 = (f32[2688]{0:T(1024)S(1)}, f32[2688]{0:T(1024)}, u32[]{:S(2)}) copy-start(f32[2688]{0:T(1024)} %param.25) | copy-start | bytes 32260
  138.7 10.2 %collective-permute-start.15 = (bf16[64,2688]{1,0:T(8,128)(2,1)S(1)}, bf16[64,2688]{1,0:T(8,128)(2,1)S(1)}, u32[]{:S(2)}, u32[]{:S(2)}) collective-permute-start(bf16[64,2688]{1,0:T(8,128)(2,1)S(1)} %fusion.20), channel_id=1, source_target_pairs={{0,2},{1,3},{2,0},{3,1},{4,6},{5,7},{6,4},{7,5},{8,10},{9,11},{10,... | collective-permute-start | bytes 1032200 | tf_op jit(solution)/shard_map/ppermute | solution.py:102
  149.1 70.3 %copy-start.3 = (f32[64,2688]{1,0:T(8,128)}, f32[64,2688]{1,0:T(8,128)S(1)}, u32[]{:S(2)}) copy-start(f32[64,2688]{1,0:T(8,128)S(1)} %get-tuple-element.56) | copy-start | bytes 2064388
  219.5 5.1 %collective-permute-start.16 = (bf16[32,16,2688]{2,1,0:T(8,128)(2,1)S(1)}, bf16[32,16,2688]{2,1,0:T(8,128)(2,1)S(1)}, u32[]{:S(2)}, u32[]{:S(2)}) collective-permute-start(bf16[32,16,2688]{2,1,0:T(8,128)(2,1)S(1)} %all_to_all.10), channel_id=1, source_target_pairs={{0,1},{1,0},{2,3},{3,2},{4,5},{5,4},{6,7},{7,6},{8,9},{9,8},{10,11... | collective-permute-start | bytes 8257544 | tf_op jit(solution)/shard_map/ppermute | solution.py:102
  246.3 7.3 %copy-start.2 = (bf16[1024,2688]{1,0:T(8,128)(2,1)S(1)}, bf16[1024,2688]{1,0:T(8,128)(2,1)}, u32[]{:S(2)}) copy-start(bf16[1024,2688]{1,0:T(8,128)(2,1)} %convolution_convert_fusion) | copy-start | bytes 16515076
  248.4 5.2 %collective-permute-start.17 = (bf16[32,16,2688]{2,1,0:T(8,128)(2,1)S(1)}, bf16[32,16,2688]{2,1,0:T(8,128)(2,1)S(1)}, u32[]{:S(2)}, u32[]{:S(2)}) collective-permute-start(bf16[32,16,2688]{2,1,0:T(8,128)(2,1)S(1)} %slice.74), channel_id=1, source_target_pairs={{0,1},{1,0},{2,3},{3,2},{4,5},{5,4},{6,7},{7,6},{8,9},{9,8},{10,11... | collective-permute-start | bytes 8257544 | tf_op jit(solution)/shard_map/ppermute | solution.py:102
  255.8 3.8 %copy-start.11 = (bf16[2688,16]{0,1:T(8,128)(2,1)S(1)}, bf16[2688,16]{0,1:T(8,128)(2,1)}, u32[]{:S(2)}) copy-start(bf16[2688,16]{0,1:T(8,128)(2,1)} %param.26) | copy-start | bytes 258052
  255.8 66.6 %all-to-all-start.1 = ((bf16[32,16,2688]{2,1,0:T(8,128)(2,1)}), bf16[32,16,2688]{2,1,0:T(8,128)(2,1)S(1)}, u32[]{:S(2)}, u32[]{:S(2)}) async-start(bf16[32,16,2688]{2,1,0:T(8,128)(2,1)} %add_convert_fusion), calls=%async_computation.1 | async-start | bytes 5505024 | tf_op jit(solution)/shard_map/all_to_all | solution.py:255
  325.8 10.0 %copy-start.1 = (bf16[256,256]{1,0:T(8,128)(2,1)S(1)}, bf16[256,256]{1,0:T(8,128)(2,1)}, u32[]{:S(2)}) copy-start(bf16[256,256]{1,0:T(8,128)(2,1)} %param.17) | copy-start | bytes 393220
  330.4 4.6 %copy-start.4 = (f32[64,2688]{1,0:T(8,128)S(1)}, f32[64,2688]{1,0:T(8,128)}, u32[]{:S(2)}) copy-start(f32[64,2688]{1,0:T(8,128)} %copy-done.3) | copy-start | bytes 2064388

commit v2 on v1

--- a/solution.py
+++ b/solution.py
@@ -1,6 +1,9 @@
+import functools
 import jax
 import jax.numpy as jnp
 from jax import lax
+from jax.experimental import pallas as pl
+from jax.experimental.pallas import tpu as pltpu
 from jax.sharding import PartitionSpec as P
 
 HEADS = 64
@@ -102,16 +105,257 @@
     return lax.ppermute(x, axis, [(i, i ^ 1 << stride) for i in range(lax.axis_size(axis))])
 
 
-def expert_half(slot_rows, up_weight, down_weight):
-    model_width = slot_rows.shape[-1]
-    flat_rows = slot_rows.reshape(-1, model_width)
-    activation = jnp.dot(flat_rows, up_weight[0], preferred_element_type=jnp.float32)
-    activation = jnp.maximum(activation, 0.0)
-    activation = (activation * activation).astype(jnp.bfloat16)
-    output = jnp.dot(activation, down_weight[0], preferred_element_type=jnp.float32).astype(
-        jnp.bfloat16
-    )
-    return output.reshape(slot_rows.shape)
+MESH = pl.DeviceIdType.MESH
+
+
+def moe_kernel(
+    planes, cols, cap, x_ref, info_ref, hidden_ref, up_hbm, down_hbm, out_ref,
+    up, down, xz, iz, pk, rows, act, own, other, back, rb, pt, fin, total,
+    weight_sem, sx, rx, si, ri, sp, rp, sf, rf, sb, rbk, sr, rr, sn, rn,
+):
+    seq, head = lax.axis_index("seq"), lax.axis_index("head")
+    wide = cols // 2
+    z, y, x, c = seq // 2, seq % 2, head // 2, head % 2
+    k = y * wide + x
+    count, width = x_ref.shape
+    tile = width // 7 if width % (7 * 128) == 0 else width
+    deep = width // 3 if width % (3 * 128) == 0 else width
+    slots = cols * cap
+
+    def in_plane(col):
+        return {"seq": 2 * z + col // wide, "head": 2 * (col % wide) + c}
+
+    def in_line(plane):
+        return {"seq": 2 * plane + y, "head": head}
+
+    mate = {"seq": seq, "head": 2 * x + 1 - c}
+
+    def remote(src, dst, send, recv, device):
+        return pltpu.make_async_remote_copy(
+            src_ref=src, dst_ref=dst, send_sem=send, recv_sem=recv,
+            device_id=device, device_id_type=MESH,
+        )
+
+    load_up = pltpu.make_async_copy(up_hbm.at[0], up, weight_sem.at[0])
+    load_down = pltpu.make_async_copy(down_hbm.at[0], down, weight_sem.at[1])
+    load_up.start()
+    load_down.start()
+
+    barrier = pltpu.get_barrier_semaphore()
+    for d in range(1, planes):
+        pl.semaphore_signal(
+            barrier, inc=1, device_id=in_line((z + d) % planes), device_id_type=MESH
+        )
+    for j in range(1, cols):
+        pl.semaphore_signal(
+            barrier, inc=1, device_id=in_plane((k + j) % cols), device_id_type=MESH
+        )
+    pl.semaphore_signal(barrier, inc=1, device_id=mate, device_id_type=MESH)
+    pl.semaphore_wait(barrier, planes + cols - 1)
+
+    def line_rows(to):
+        return remote(x_ref, xz.at[z], sx.at[to], rx.at[z], in_line(to))
+
+    def line_info(to):
+        return remote(info_ref.at[to], iz.at[z], si.at[to], ri.at[z], in_line(to))
+
+    def spread(block, col):
+        part = pl.ds(pl.multiple_of(col * cap, cap), cap)
+        place = pl.ds(pl.multiple_of(k * cap, cap), cap)
+        return remote(
+            pk.at[block, part], rows.at[block, 0, place],
+            sp.at[block, col], rp.at[block, k], in_plane(col),
+        )
+
+    def forward(block):
+        return remote(rows.at[block, 0], rows.at[block, 1], sf.at[block], rf.at[block], mate)
+
+    def half_back(block):
+        return remote(other.at[block], back.at[block], sb.at[block], rbk.at[block], mate)
+
+    def give_back(block, col):
+        part = pl.ds(pl.multiple_of(col * cap, cap), cap)
+        place = pl.ds(pl.multiple_of(k * cap, cap), cap)
+        return remote(
+            own.at[block, part], rb.at[block, place],
+            sr.at[block, col], rr.at[block, k], in_plane(col),
+        )
+
+    def line_back(to):
+        return remote(pt.at[to], fin.at[z], sn.at[to], rn.at[z], in_line(to))
+
+    def got(dst, sem):
+        pltpu.make_async_copy(dst, dst, sem).wait()
+
+    for d in range(1, planes):
+        line_rows((z + d) % planes).start()
+        line_info((z + d) % planes).start()
+
+    mine = pl.ds(pl.multiple_of(k * cap, cap), cap)
+
+    def pack(d):
+        block = (z + planes - d) % planes
+
+        @pl.when(d == 0)
+        def _():
+            xz[z] = x_ref[...]
+            iz[z] = info_ref[z]
+
+        @pl.when(d > 0)
+        def _():
+            got(xz.at[block], rx.at[block])
+            got(iz.at[block], ri.at[block])
+
+        pk[block] = lax.dot_general(
+            iz[block, pl.ds(0, count)], xz[block], (((0,), (0,)), ((), ())),
+            preferred_element_type=jnp.float32,
+        ).astype(jnp.bfloat16)
+        for j in range(1, cols):
+            spread(block, (k + j) % cols).start()
+        rows[block, 0, mine] = pk[block, mine]
+
+    def pass_on(d):
+        block = (z + planes - d) % planes
+        for j in range(1, cols):
+            col = (k + j) % cols
+            place = pl.ds(pl.multiple_of(col * cap, cap), cap)
+            got(rows.at[block, 0, place], rp.at[block, col])
+        forward(block).start()
+
+    def compute(d):
+        block = (z + planes - d) % planes
+
+        @pl.when(d == 0)
+        def _():
+            load_up.wait()
+            load_down.wait()
+
+        got(rows.at[block, 1], rf.at[block])
+        total[...] = jnp.zeros_like(total)
+
+        def gather_up(i, carry):
+            at = pl.ds(pl.multiple_of(i * deep, 128), deep)
+            taken = rows[block, :, :, at].reshape(2 * slots, deep)
+            total[...] += jnp.dot(taken, up[at, :], preferred_element_type=jnp.float32)
+            return carry
+
+        lax.fori_loop(0, width // deep, gather_up, 0)
+        kept = jnp.maximum(total[...], 0.0)
+        act[...] = (kept * kept).astype(jnp.bfloat16)
+
+        def gather_down(i, carry):
+            at = pl.ds(pl.multiple_of(i * tile, 128), tile)
+            result = jnp.dot(act[...], down[:, at], preferred_element_type=jnp.float32)
+            result = result.astype(jnp.bfloat16)
+            own[block, :, at] = result[:slots]
+            other[block, :, at] = result[slots:]
+            return carry
+
+        lax.fori_loop(0, width // tile, gather_down, 0)
+        half_back(block).start()
+
+    def add_halves(d):
+        block = (z + planes - d) % planes
+        got(back.at[block], rbk.at[block])
+        own[block] = (
+            own[block].astype(jnp.float32) + back[block].astype(jnp.float32)
+        ).astype(jnp.bfloat16)
+        for j in range(1, cols):
+            give_back(block, (k + j) % cols).start()
+        rb[block, mine] = own[block, mine]
+
+    def combine(d):
+        block = (z + planes - d) % planes
+        for j in range(1, cols):
+            col = (k + j) % cols
+            place = pl.ds(pl.multiple_of(col * cap, cap), cap)
+            got(rb.at[block, place], rr.at[block, col])
+        pt[block] = jnp.dot(
+            iz[block, pl.ds(count, count)], rb[block], preferred_element_type=jnp.float32
+        ).astype(jnp.bfloat16)
+
+        @pl.when(d > 0)
+        def _():
+            line_back(block).start()
+
+    def step(t, carry):
+        for lag, stage in ((0, pack), (2, compute), (1, pass_on), (3, add_halves), (4, combine)):
+
+            @pl.when((t >= lag) & (t < planes + lag))
+            def _(lag=lag, stage=stage):
+                stage(t - lag)
+
+        return carry
+
+    lax.fori_loop(0, planes + 4, step, 0)
+
+    answer = hidden_ref[...] + pt[z].astype(jnp.float32)
+    for d in range(1, planes):
+        block = (z + planes - d) % planes
+        got(fin.at[block], rn.at[block])
+        answer += fin[block].astype(jnp.float32)
+    out_ref[...] = answer.astype(out_ref.dtype)
+
+    for d in range(1, planes):
+        to = (z + d) % planes
+        line_rows(to).wait_send()
+        line_info(to).wait_send()
+        line_back(to).wait_send()
+
+    def finish(block, carry):
+        for j in range(1, cols):
+            spread(block, (k + j) % cols).wait_send()
+            give_back(block, (k + j) % cols).wait_send()
+        forward(block).wait_send()
+        half_back(block).wait_send()
+        return carry
+
+    lax.fori_loop(0, planes, finish, 0)
+
+
+def expert_layer(inputs, info, hidden, up_weight, down_weight, planes, cols, cap):
+    count, width = inputs.shape
+    units = up_weight.shape[2]
+    slots = cols * cap
+    dma = pltpu.SemaphoreType.DMA
+    bf16 = jnp.bfloat16
+    vmem = pl.BlockSpec(memory_space=pltpu.VMEM)
+    return pl.pallas_call(
+        functools.partial(moe_kernel, planes, cols, cap),
+        out_shape=jax.ShapeDtypeStruct((count, width), bf16),
+        in_specs=[vmem, vmem, vmem, pl.BlockSpec(memory_space=pl.ANY), pl.BlockSpec(memory_space=pl.ANY)],
+        out_specs=vmem,
+        scratch_shapes=[
+            pltpu.VMEM((width, units), bf16),
+            pltpu.VMEM((units, width), bf16),
+            pltpu.VMEM((planes, count, width), bf16),
+            pltpu.VMEM((planes, 2 * count, slots), bf16),
+            pltpu.VMEM((planes, slots, width), bf16),
+            pltpu.VMEM((planes, 2, slots, width), bf16),
+            pltpu.VMEM((2 * slots, units), bf16),
+            pltpu.VMEM((planes, slots, width), bf16),
+            pltpu.VMEM((planes, slots, width), bf16),
+            pltpu.VMEM((planes, slots, width), bf16),
+            pltpu.VMEM((planes, slots, width), bf16),
+            pltpu.VMEM((planes, count, width), bf16),
+            pltpu.VMEM((planes, count, width), bf16),
+            pltpu.VMEM((2 * slots, units), jnp.float32),
+            dma((2,)),
+            dma((planes,)), dma((planes,)), dma((planes,)), dma((planes,)),
+            dma((planes, cols)), dma((planes, cols)),
+            dma((planes,)), dma((planes,)), dma((planes,)), dma((planes,)),
+            dma((planes, cols)), dma((planes, cols)),
+            dma((planes,)), dma((planes,)),
+        ],
+        compiler_params=pltpu.CompilerParams(
+            collective_id=1, has_side_effects=True, vmem_limit_bytes=60 * 1024 * 1024
+        ),
+        cost_estimate=pl.CostEstimate(
+            flops=8 * planes * slots * width * units,
+            bytes_accessed=4 * width * units,
+            transcendentals=0,
+        ),
+    )(inputs, info, hidden, up_weight, down_weight)
 
 
 def per_device(
@@ -234,33 +478,16 @@
     flat_hits = expert_hits.astype(jnp.int32).reshape(rows_own * TOP, experts)
     before = jnp.cumsum(flat_hits, axis=0) - flat_hits
     slot_index = jnp.sum(before * flat_hits, axis=1)
-    target = expert_index.reshape(rows_own * TOP) * capacity + slot_index
-    placing = jnp.arange(experts * capacity, dtype=jnp.int32)[:, None] == target[None, :]
-    placing = jnp.any(placing.reshape(experts * capacity, rows_own, TOP), axis=2).astype(
-        jnp.bfloat16
-    )
-    outgoing = jnp.dot(placing, inputs, preferred_element_type=jnp.float32).astype(jnp.bfloat16)
-    outgoing = outgoing.reshape(experts, capacity, model_width)
-    halves = outgoing.reshape(experts, 2, capacity // 2, model_width).reshape(
-        2 * experts, capacity // 2, model_width
-    )
-    slot_rows = lax.all_to_all(halves, ("seq", "head"), split_axis=0, concat_axis=0, tiled=True)
-    other_rows = partner(slot_rows, "head", 0)
-    both_rows = jnp.concatenate([slot_rows, other_rows], axis=1)
-    both_parts = expert_half(both_rows, up_weight, down_weight)
-    own_part = both_parts[:, : slot_rows.shape[1]]
-    other_part = both_parts[:, slot_rows.shape[1] :]
-    back_part = partner(other_part, "head", 0)
-    summed = (own_part.astype(jnp.float32) + back_part.astype(jnp.float32)).astype(jnp.bfloat16)
-    returned = lax.all_to_all(summed, ("seq", "head"), split_axis=0, concat_axis=0, tiled=True)
-    results = returned.reshape(experts, 2, capacity // 2, model_width).reshape(
-        experts, capacity, model_width
-    )
-    gathered = results.reshape(experts * capacity, model_width)[target].reshape(
-        rows_own, TOP, model_width
-    )
-    moe_out = jnp.sum(shares[:, :, None] * gathered.astype(jnp.float32), axis=1)
-    return (hidden + moe_out).astype(jnp.bfloat16)
+    cols = lax.axis_size("head")
+    planes = lax.axis_size("seq") // 2
+    cap = -(-capacity // 16) * 16
+    target = expert_index * cap + slot_index.reshape(rows_own, TOP)
+    chosen = target[:, :, None] == jnp.arange(experts * cap, dtype=jnp.int32)[None, None, :]
+    place = jnp.any(chosen, axis=1).astype(jnp.bfloat16)
+    weigh = jnp.sum(jnp.where(chosen, shares[:, :, None], 0.0), axis=1).astype(jnp.bfloat16)
+    info = jnp.concatenate([place, weigh], axis=0)
+    info = info.reshape(2 * rows_own, planes, cols * cap).transpose(1, 0, 2)
+    return expert_layer(inputs, info, hidden, up_weight, down_weight, planes, cols, cap)
 
 
 def solution(mesh):

time: 337 us -> 257 us (0.76)
  Pallas kernels: 0 us -> 99.8 us
  waiting for transfers between devices: 143 us -> 70.8 us
  blocking collectives: 69.3 us -> 0 us
  matrix products: 29.5 us -> 8.49 us
  other arithmetic: 21.7 us -> 11.1 us
  starting transfers between devices: 51.5 us -> 45.3 us
    pallas_call x0 -> x1, Pallas kernels: none -> 99.8 us  [expert_layer(): pl.pallas_call(functools.partial(moe_kernel, planes, cols, cap), out_shap...]
    all_to_all x1 -> x0, blocking collectives: 69.3 us -> none  [per_device(): lax.all_to_all(halves, ('seq', 'head'), split_axis=0, concat_axis=0, tile...]
    all_to_all x1 -> x0, waiting for transfers between devices: 61.3 us -> none  [per_device(): lax.all_to_all(summed, ('seq', 'head'), split_axis=0, concat_axis=0, tile...]
    dot_general x2 -> x0, matrix products: 19.9 us -> none  [the longest x1 18.9 us: expert_half(): jnp.dot(activation, down_weight[0], preferred_element_type=jnp.float32)]
    unnamed x35 -> x33, local copies, waits for them, and re-layouts: 1.63 us -> 11.4 us
    ppermute x9 -> x7, waiting for transfers between devices: 51.8 us -> 44.4 us  [partner(): lax.ppermute(x, axis, [(i, i ^ 1 << stride) for i in range(lax.axis_size(...]
    convert_element_type x1, local copies, waits for them, and re-layouts: 4.59 us -> 0.01 us  [per_device(): jnp.sum(jnp.where(chosen, shares[:, :, None], 0.0), axis=1)]
    reduce_sum x1, other arithmetic: 4.56 us -> 0.19 us  [per_device(): jnp.sum(jnp.where(chosen, shares[:, :, None], 0.0), axis=1)]
  transfers between devices with their start and end apart: 19 -> 16, of which waited for: 12 -> 9; matrix products, arithmetic and copies ran while one was open for 6% -> 10% of each run, Pallas kernels for 0% -> 0%
where the time goes in v2:
time: 257 us; the launch traced here: 256 us
  Pallas kernels  99.8 us (39%)
  waiting for transfers between devices  70.8 us (28%)
  starting transfers between devices  45.3 us (18%)
  local copies, waits for them, and re-layouts  19.5 us (8%)
  other arithmetic  11.1 us (4%)
  matrix products  8.49 us (3%)
    pallas_call x1, Pallas kernels, expert_layer(): pl.pallas_call(functools.partial(moe_kernel, planes, cols, cap), out_shap...  99.8 us
    ppermute x7, waiting for transfers between devices, partner(): lax.ppermute(x, axis, [(i, i ^ 1 << stride) for i in range(lax.axis_size(...  44.4 us
    ppermute x9, starting transfers between devices, shift(): return lax.ppermute(x, axis, pairs)  34.4 us
    ppermute x9, waiting for transfers between devices, shift(): return lax.ppermute(x, axis, pairs)  26.4 us
    unnamed x33, local copies, waits for them, and re-layouts  11.4 us
    ppermute x7, starting transfers between devices, partner(): lax.ppermute(x, axis, [(i, i ^ 1 << stride) for i in range(lax.axis_size(...  10.9 us
    dot_general x8, matrix products, project(): jnp.dot(normed, block, preferred_element_type=jnp.float32)  5.26 us
  transfers between devices with their start and end apart: 16, of which 9 were waited for; matrix products, arithmetic and copies ran while one was open for 10% of the time, Pallas kernels for 0%

profile of v2, /device:TPU:0, one launch (start us, length us, event | category | flops | bytes accessed | tf_op | source)
XLA Modules:
  0.0 255.8 jit_solution(10285664052920027816)
XLA Ops:
  0.0 0.7 multiply_exponential_fusion
  0.7 0.8 copy_bitcast_fusion.5
  1.5 0.6 reduce-window.14
  2.5 0.8 exponential_multiply_fusion
  3.4 1.2 copy.104
  5.3 3.0 %collective-permute-start = (bf16[16,72,128]{2,1,0:T(8,128)(2,1)S(1)}, bf16[16,72,128]{2,1,0:T(8,128)(2,1)S(1)}, u32[]{:S(2)}, u32[]{:S(2)}) collective-permute-start(bf16[16,72,128]{2,1,0:T(8,128)(2,1)S(1)} %pad_maximum_fusion), channel_id=1, source_target_pairs={{0,4},{4,0},{8,12},{12,8},{16,20},{20,16},{24,28},{28,24},{1,5},{5... | collective-permute-start | bytes 884744 | tf_op jit(solution)/shard_map/ppermute | solution.py:105
  8.3 7.0 %collective-permute-done = bf16[16,72,128]{2,1,0:T(8,128)(2,1)S(1)} collective-permute-done((bf16[16,72,128]{2,1,0:T(8,128)(2,1)S(1)}, bf16[16,72,128]{2,1,0:T(8,128)(2,1)S(1)}, u32[]{:S(2)}, u32[]{:S(2)}) %collective-permute-start) | collective-permute-done | bytes 294944 | tf_op jit(solution)/shard_map/ppermute | solution.py:105
  16.1 3.7 %collective-permute-start.1 = (bf16[16,72,128]{2,1,0:T(8,128)(2,1)S(1)}, bf16[16,72,128]{2,1,0:T(8,128)(2,1)S(1)}, u32[]{:S(2)}, u32[]{:S(2)}) collective-permute-start(bf16[16,72,128]{2,1,0:T(8,128)(2,1)S(1)} %pad_maximum_fusion.1), channel_id=1, source_target_pairs={{0,8},{4,12},{8,16},{12,20},{16,24},{20,28},{1,9},{5,13},{9,17},{1... | collective-permute-start | bytes 884744 | tf_op jit(solution)/shard_map/ppermute | solution.py:24
  19.8 1.3 collective-permute-start.5
  21.1 5.4 %collective-permute-start.6 = (bf16[1024,336]{0,1:T(8,128)(2,1)}, bf16[1024,336]{0,1:T(8,128)(2,1)}, u32[]{:S(2)}, u32[]{:S(2)}) collective-permute-start(bf16[1024,336]{0,1:T(8,128)(2,1)} %param.23), channel_id=1, source_target_pairs={{0,8},{4,12},{8,16},{12,20},{16,24},{20,28},{1,9},{5,13},{9,17},{1... | collective-permute-start | bytes 2064392 | tf_op jit(solution)/shard_map/ppermute | solution.py:24
  26.6 1.5 collective-permute-start.4
  28.1 1.2 copy.110
  30.2 2.7 %collective-permute-start.2 = (bf16[16,72,128]{2,1,0:T(8,128)(2,1)S(1)}, bf16[16,72,128]{2,1,0:T(8,128)(2,1)S(1)}, u32[]{:S(2)}, u32[]{:S(2)}) collective-permute-start(bf16[16,72,128]{2,1,0:T(8,128)(2,1)S(1)} %pad_maximum_fusion.2), channel_id=1, source_target_pairs={{0,8},{4,12},{8,16},{12,20},{16,24},{20,28},{1,9},{5,13},{9,17},{1... | collective-permute-start | bytes 884744 | tf_op jit(solution)/shard_map/ppermute | solution.py:24
  32.9 1.2 fusion.2
  34.1 12.1 %collective-permute-done.2 = bf16[16,72,128]{2,1,0:T(8,128)(2,1)S(1)} collective-permute-done((bf16[16,72,128]{2,1,0:T(8,128)(2,1)S(1)}, bf16[16,72,128]{2,1,0:T(8,128)(2,1)S(1)}, u32[]{:S(2)}, u32[]{:S(2)}) %collective-permute-start.2) | collective-permute-done | bytes 294944 | tf_op jit(solution)/shard_map/ppermute | solution.py:24
  46.8 5.5 %collective-permute-start.3 = (bf16[16,72,128]{2,1,0:T(8,128)(2,1)S(1)}, bf16[16,72,128]{2,1,0:T(8,128)(2,1)S(1)}, u32[]{:S(2)}, u32[]{:S(2)}) collective-permute-start(bf16[16,72,128]{2,1,0:T(8,128)(2,1)S(1)} %pad_maximum_fusion.3), channel_id=1, source_target_pairs={{0,16},{4,20},{8,24},{12,28},{1,17},{5,21},{9,25},{13,29},{2,18},{... | collective-permute-start | bytes 884744 | tf_op jit(solution)/shard_map/ppermute | solution.py:24
  52.3 0.8 convolution_bitcast_fusion
  53.1 1.3 collective-permute-start.10
  54.4 5.4 %collective-permute-start.7 = (bf16[1024,336]{0,1:T(8,128)(2,1)}, bf16[1024,336]{0,1:T(8,128)(2,1)}, u32[]{:S(2)}, u32[]{:S(2)}) collective-permute-start(bf16[1024,336]{0,1:T(8,128)(2,1)} %collective-permute-done.6), channel_id=1, source_target_pairs={{0,8},{4,12},{8,16},{12,20},{16,24},{20,28},{1,9},{5,13},{9,17},{1... | collective-permute-start | bytes 2064392 | tf_op jit(solution)/shard_map/ppermute | solution.py:24
  60.0 1.8 fusion.9
  62.5 1.6 copy.109
  64.1 0.5 multiply_convert_fusion
  64.6 6.0 %collective-permute-done.10 = bf16[1024,336]{0,1:T(8,128)(2,1)} collective-permute-done((bf16[1024,336]{0,1:T(8,128)(2,1)}, bf16[1024,336]{0,1:T(8,128)(2,1)}, u32[]{:S(2)}, u32[]{:S(2)}) %collective-permute-start.10) | collective-permute-done | bytes 688160 | tf_op jit(solution)/shard_map/ppermute | solution.py:24
  70.6 1.3 collective-permute-start.12
  71.9 1.5 convolution_convert_fusion.6
  73.4 7.7 %collective-permute-start.8 = (bf16[1024,336]{0,1:T(8,128)(2,1)}, bf16[1024,336]{0,1:T(8,128)(2,1)S(1)}, u32[]{:S(2)}, u32[]{:S(2)}) collective-permute-start(bf16[1024,336]{0,1:T(8,128)(2,1)} %collective-permute-done.7), channel_id=1, source_target_pairs={{0,8},{4,12},{8,16},{12,20},{16,24},{20,28},{1,9},{5,13},{9,17},{1... | collective-permute-start | bytes 2064392 | tf_op jit(solution)/shard_map/ppermute | solution.py:24
  81.2 1.2 broadcast_select_fusion.1
  82.4 1.6 collective-permute-start.11
  83.9 1.5 broadcast_select_fusion.10
  85.5 1.7 collective-permute-done.12
  87.2 1.6 collective-permute-start.13
  88.8 6.6 %collective-permute-done.8 = bf16[1024,336]{0,1:T(8,128)(2,1)S(1)} collective-permute-done((bf16[1024,336]{0,1:T(8,128)(2,1)}, bf16[1024,336]{0,1:T(8,128)(2,1)S(1)}, u32[]{:S(2)}, u32[]{:S(2)}) %collective-permute-start.8) | collective-permute-done | bytes 688160 | tf_op jit(solution)/shard_map/ppermute | solution.py:24
  95.4 1.2 broadcast_select_fusion.2
  96.6 1.6 collective-permute-start.9
  98.2 2.6 %collective-permute-done.11 = bf16[1024,336]{0,1:T(8,128)(2,1)S(1)} collective-permute-done((bf16[1024,336]{0,1:T(8,128)(2,1)S(1)}, bf16[1024,336]{0,1:T(8,128)(2,1)S(1)}, u32[]{:S(2)}, u32[]{:S(2)}) %collective-permute-start.11) | collective-permute-done | bytes 688160 | tf_op jit(solution)/shard_map/ppermute | solution.py:105
  101.2 0.4 broadcast_select_fusion.6
  101.6 14.0 %collective-permute-done.13 = bf16[1024,336]{0,1:T(8,128)(2,1)S(1)} collective-permute-done((bf16[1024,336]{0,1:T(8,128)(2,1)S(1)}, bf16[1024,336]{0,1:T(8,128)(2,1)S(1)}, u32[]{:S(2)}, u32[]{:S(2)}) %collective-permute-start.13) | collective-permute-done | bytes 688160 | tf_op jit(solution)/shard_map/ppermute | solution.py:105
  116.3 12.0 %collective-permute-done.9 = bf16[1024,336]{0,1:T(8,128)(2,1)S(1)} collective-permute-done((bf16[1024,336]{0,1:T(8,128)(2,1)S(1)}, bf16[1024,336]{0,1:T(8,128)(2,1)S(1)}, u32[]{:S(2)}, u32[]{:S(2)}) %collective-permute-start.9) | collective-permute-done | bytes 688160 | tf_op jit(solution)/shard_map/ppermute | solution.py:105
  128.3 0.4 convolution_convert_fusion.5
  129.4 1.3 copy.112
  130.7 1.2 reshape_reshape.3
  132.4 0.9 reduce-window.16
  133.8 8.1 %copy.120.up_hbm = bf16[1,2688,928]{2,1,0:T(8,128)(2,1)} copy(bf16[1,2688,928]{1,2,0:T(8,128)(2,1)} %param.28) | data formatting | bytes 9977856 | tf_op args[13]
  142.1 1.5 collective-permute-start.15
  143.9 8.8 %collective-permute-done.15 = bf16[64,2688]{1,0:T(8,128)(2,1)S(1)} collective-permute-done((bf16[64,2688]{1,0:T(8,128)(2,1)S(1)}, bf16[64,2688]{1,0:T(8,128)(2,1)S(1)}, u32[]{:S(2)}, u32[]{:S(2)}) %collective-permute-start.15) | collective-permute-done | bytes 344096 | tf_op jit(solution)/shard_map/ppermute | solution.py:105
  153.6 0.6 maximum_bitcast_fusion.4.info_ref
  154.2 99.8 %shard_map.145 = bf16[64,2688]{1,0:T(8,128)(2,1)} custom-call(bf16[64,2688]{1,0:T(8,128)(2,1)} %copy-done.4, bf16[4,128,128]{2,1,0:T(8,128)(2,1)} %maximum_bitcast_fusion.4.info_ref, f32[64,2688]{1,0:T(8,128)} %copy-done.1, bf16[1,2688,928]{2,1,0:T(8,128)(2,1)} %copy.120.up_hbm, bf16[1,928,2688]{2,1,0:T(8,128)(2,1)} %down_hbm.1), custom_call_target="tpu_custom_call" | custom-call | flops 10217324544 | bytes 9977856 | tf_op jit(solution)/shard_map/pallas_call | solution.py:323
  254.1 1.7 copy.152
  (114 shorter events, 8.3 us)
Async XLA Ops:
  0.0 4.6 %copy-start = (bf16[256,256]{1,0:T(8,128)(2,1)S(1)}, bf16[256,256]{1,0:T(8,128)(2,1)}, u32[]{:S(2)}) copy-start(bf16[256,256]{1,0:T(8,128)(2,1)} %param.17) | copy-start | bytes 393220
  4.8 23.2 %copy-start.2 = (bf16[256,1024]{1,0:T(8,128)(2,1)S(1)}, bf16[256,1024]{1,0:T(8,128)(2,1)}, u32[]{:S(2)}) copy-start(bf16[256,1024]{1,0:T(8,128)(2,1)} %param.16) | copy-start | bytes 1572868
  5.3 24.0 %copy-start.13 = (f32[16]{0:T(128)S(1)}, f32[16]{0:T(128)}, u32[]{:S(2)}) copy-start(f32[16]{0:T(128)} %param.21) | copy-start | bytes 196
  5.3 24.2 %copy-start.6 = (bf16[256,256]{1,0:T(8,128)(2,1)S(1)}, bf16[256,256]{1,0:T(8,128)(2,1)}, u32[]{:S(2)}) copy-start(bf16[256,256]{1,0:T(8,128)(2,1)} %param.18) | copy-start | bytes 393220
  5.3 10.0 %collective-permute-start = (bf16[16,72,128]{2,1,0:T(8,128)(2,1)S(1)}, bf16[16,72,128]{2,1,0:T(8,128)(2,1)S(1)}, u32[]{:S(2)}, u32[]{:S(2)}) collective-permute-start(bf16[16,72,128]{2,1,0:T(8,128)(2,1)S(1)} %pad_maximum_fusion), channel_id=1, source_target_pairs={{0,4},{4,0},{8,12},{12,8},{16,20},{20,16},{24,28},{28,24},{1,5},{5... | collective-permute-start | bytes 884744 | tf_op jit(solution)/shard_map/ppermute | solution.py:105
  16.1 16.8 %copy-start.8 = (f32[256,16]{0,1:T(8,128)S(1)}, f32[256,16]{0,1:T(8,128)}, u32[]{:S(2)}) copy-start(f32[256,16]{0,1:T(8,128)} %param.19) | copy-start | bytes 49156
  16.1 13.6 %collective-permute-start.1 = (bf16[16,72,128]{2,1,0:T(8,128)(2,1)S(1)}, bf16[16,72,128]{2,1,0:T(8,128)(2,1)S(1)}, u32[]{:S(2)}, u32[]{:S(2)}) collective-permute-start(bf16[16,72,128]{2,1,0:T(8,128)(2,1)S(1)} %pad_maximum_fusion.1), channel_id=1, source_target_pairs={{0,8},{4,12},{8,16},{12,20},{16,24},{20,28},{1,9},{5,13},{9,17},{1... | collective-permute-start | bytes 884744 | tf_op jit(solution)/shard_map/ppermute | solution.py:24
  19.8 33.2 %collective-permute-start.5 = (bf16[1024,336]{0,1:T(8,128)(2,1)}, bf16[1024,336]{0,1:T(8,128)(2,1)}, u32[]{:S(2)}, u32[]{:S(2)}) collective-permute-start(bf16[1024,336]{0,1:T(8,128)(2,1)} %param.23), channel_id=1, source_target_pairs={{8,0},{12,4},{16,8},{20,12},{24,16},{28,20},{9,1},{13,5},{17,9},{2... | collective-permute-start | bytes 2064392 | tf_op jit(solution)/shard_map/ppermute | solution.py:24
  21.1 33.3 %collective-permute-start.6 = (bf16[1024,336]{0,1:T(8,128)(2,1)}, bf16[1024,336]{0,1:T(8,128)(2,1)}, u32[]{:S(2)}, u32[]{:S(2)}) collective-permute-start(bf16[1024,336]{0,1:T(8,128)(2,1)} %param.23), channel_id=1, source_target_pairs={{0,8},{4,12},{8,16},{12,20},{16,24},{20,28},{1,9},{5,13},{9,17},{1... | collective-permute-start | bytes 2064392 | tf_op jit(solution)/shard_map/ppermute | solution.py:24
  26.6 57.4 %collective-permute-start.4 = (bf16[1024,336]{0,1:T(8,128)(2,1)}, bf16[1024,336]{0,1:T(8,128)(2,1)}, u32[]{:S(2)}, u32[]{:S(2)}) collective-permute-start(bf16[1024,336]{0,1:T(8,128)(2,1)} %param.23), channel_id=1, source_target_pairs={{0,4},{4,0},{8,12},{12,8},{16,20},{20,16},{24,28},{28,24},{1,5},{5... | collective-permute-start | bytes 2064392 | tf_op jit(solution)/shard_map/ppermute | solution.py:105
  30.2 16.1 %collective-permute-start.2 = (bf16[16,72,128]{2,1,0:T(8,128)(2,1)S(1)}, bf16[16,72,128]{2,1,0:T(8,128)(2,1)S(1)}, u32[]{:S(2)}, u32[]{:S(2)}) collective-permute-start(bf16[16,72,128]{2,1,0:T(8,128)(2,1)S(1)} %pad_maximum_fusion.2), channel_id=1, source_target_pairs={{0,8},{4,12},{8,16},{12,20},{16,24},{20,28},{1,9},{5,13},{9,17},{1... | collective-permute-start | bytes 884744 | tf_op jit(solution)/shard_map/ppermute | solution.py:24
  46.7 13.2 %copy-start.5 = (f32[256,1024]{0,1:T(8,128)S(1)}, f32[256,1024]{0,1:T(8,128)}, u32[]{:S(2)}) copy-start(f32[256,1024]{0,1:T(8,128)} %copy.110) | copy-start | bytes 3145732
  46.8 13.0 %collective-permute-start.3 = (bf16[16,72,128]{2,1,0:T(8,128)(2,1)S(1)}, bf16[16,72,128]{2,1,0:T(8,128)(2,1)S(1)}, u32[]{:S(2)}, u32[]{:S(2)}) collective-permute-start(bf16[16,72,128]{2,1,0:T(8,128)(2,1)S(1)} %pad_maximum_fusion.3), channel_id=1, source_target_pairs={{0,16},{4,20},{8,24},{12,28},{1,17},{5,21},{9,25},{13,29},{2,18},{... | collective-permute-start | bytes 884744 | tf_op jit(solution)/shard_map/ppermute | solution.py:24
  53.1 17.5 %collective-permute-start.10 = (bf16[1024,336]{0,1:T(8,128)(2,1)}, bf16[1024,336]{0,1:T(8,128)(2,1)}, u32[]{:S(2)}, u32[]{:S(2)}) collective-permute-start(bf16[1024,336]{0,1:T(8,128)(2,1)} %collective-permute-done.5), channel_id=1, source_target_pairs={{8,0},{12,4},{16,8},{20,12},{24,16},{28,20},{9,1},{13,5},{17,9},{2... | collective-permute-start | bytes 2064392 | tf_op jit(solution)/shard_map/ppermute | solution.py:24
  54.4 19.0 %collective-permute-start.7 = (bf16[1024,336]{0,1:T(8,128)(2,1)}, bf16[1024,336]{0,1:T(8,128)(2,1)}, u32[]{:S(2)}, u32[]{:S(2)}) collective-permute-start(bf16[1024,336]{0,1:T(8,128)(2,1)} %collective-permute-done.6), channel_id=1, source_target_pairs={{0,8},{4,12},{8,16},{12,20},{16,24},{20,28},{1,9},{5,13},{9,17},{1... | collective-permute-start | bytes 2064392 | tf_op jit(solution)/shard_map/ppermute | solution.py:24
  62.0 2.1 copy-start.3
  62.0 2.1 copy-start.12
  70.6 16.5 %collective-permute-start.12 = (bf16[1024,336]{0,1:T(8,128)(2,1)}, bf16[1024,336]{0,1:T(8,128)(2,1)S(1)}, u32[]{:S(2)}, u32[]{:S(2)}) collective-permute-start(bf16[1024,336]{0,1:T(8,128)(2,1)} %collective-permute-done.10), channel_id=1, source_target_pairs={{8,0},{12,4},{16,8},{20,12},{24,16},{28,20},{9,1},{13,5},{17,9},{2... | collective-permute-start | bytes 2064392 | tf_op jit(solution)/shard_map/ppermute | solution.py:24
  73.4 22.0 %collective-permute-start.8 = (bf16[1024,336]{0,1:T(8,128)(2,1)}, bf16[1024,336]{0,1:T(8,128)(2,1)S(1)}, u32[]{:S(2)}, u32[]{:S(2)}) collective-permute-start(bf16[1024,336]{0,1:T(8,128)(2,1)} %collective-permute-done.7), channel_id=1, source_target_pairs={{0,8},{4,12},{8,16},{12,20},{16,24},{20,28},{1,9},{5,13},{9,17},{1... | collective-permute-start | bytes 2064392 | tf_op jit(solution)/shard_map/ppermute | solution.py:24
  82.4 18.4 %collective-permute-start.11 = (bf16[1024,336]{0,1:T(8,128)(2,1)S(1)}, bf16[1024,336]{0,1:T(8,128)(2,1)S(1)}, u32[]{:S(2)}, u32[]{:S(2)}) collective-permute-start(bf16[1024,336]{0,1:T(8,128)(2,1)S(1)} %broadcast_select_fusion.1), channel_id=1, source_target_pairs={{0,4},{4,0},{8,12},{12,8},{16,20},{20,16},{24,28},{28,24},{1,5},{5... | collective-permute-start | bytes 2064392 | tf_op jit(solution)/shard_map/ppermute | solution.py:105
  87.2 28.3 %collective-permute-start.13 = (bf16[1024,336]{0,1:T(8,128)(2,1)S(1)}, bf16[1024,336]{0,1:T(8,128)(2,1)S(1)}, u32[]{:S(2)}, u32[]{:S(2)}) collective-permute-start(bf16[1024,336]{0,1:T(8,128)(2,1)S(1)} %broadcast_select_fusion), channel_id=1, source_target_pairs={{0,4},{4,0},{8,12},{12,8},{16,20},{20,16},{24,28},{28,24},{1,5},{5... | collective-permute-start | bytes 2064392 | tf_op jit(solution)/shard_map/ppermute | solution.py:105
  96.6 31.7 %collective-permute-start.9 = (bf16[1024,336]{0,1:T(8,128)(2,1)S(1)}, bf16[1024,336]{0,1:T(8,128)(2,1)S(1)}, u32[]{:S(2)}, u32[]{:S(2)}) collective-permute-start(bf16[1024,336]{0,1:T(8,128)(2,1)S(1)} %broadcast_select_fusion.2), channel_id=1, source_target_pairs={{0,4},{4,0},{8,12},{12,8},{16,20},{20,16},{24,28},{28,24},{1,5},{5... | collective-permute-start | bytes 2064392 | tf_op jit(solution)/shard_map/ppermute | solution.py:105
  130.6 1.4 copy-start.10
  131.9 10.0 %collective-permute-start.14 = (bf16[2,64,2688]{2,1,0:T(8,128)(2,1)S(1)}, bf16[2,64,2688]{2,1,0:T(8,128)(2,1)S(1)}, u32[]{:S(2)}, u32[]{:S(2)}) collective-permute-start(bf16[2,64,2688]{2,1,0:T(8,128)(2,1)S(1)} %dynamic-slice_bitcast_fusion.1), channel_id=1, source_target_pairs={{0,1},{1,0},{2,3},{3,2},{4,5},{5,4},{6,7},{7,6},{8,9},{9,8},{10,11... | collective-permute-start | bytes 2064392 | tf_op jit(solution)/shard_map/ppermute | solution.py:105
  141.9 10.8 %copy-start.7 = (bf16[64,2688]{1,0:T(8,128)(2,1)S(1)}, bf16[64,2688]{1,0:T(8,128)(2,1)}, u32[]{:S(2)}) copy-start(bf16[64,2688]{1,0:T(8,128)(2,1)} %param.24) | copy-start | bytes 1032196
  141.9 11.0 %copy-start.11 = (f32[2688]{0:T(1024)S(1)}, f32[2688]{0:T(1024)}, u32[]{:S(2)}) copy-start(f32[2688]{0:T(1024)} %param.25) | copy-start | bytes 32260
  142.1 11.0 %copy-start.9 = (bf16[2688,16]{0,1:T(8,128)(2,1)S(1)}, bf16[2688,16]{0,1:T(8,128)(2,1)}, u32[]{:S(2)}) copy-start(bf16[2688,16]{0,1:T(8,128)(2,1)} %param.26) | copy-start | bytes 258052
  142.1 10.5 %collective-permute-start.15 = (bf16[64,2688]{1,0:T(8,128)(2,1)S(1)}, bf16[64,2688]{1,0:T(8,128)(2,1)S(1)}, u32[]{:S(2)}, u32[]{:S(2)}) collective-permute-start(bf16[64,2688]{1,0:T(8,128)(2,1)S(1)} %fusion.15), channel_id=1, source_target_pairs={{0,2},{1,3},{2,0},{3,1},{4,6},{5,7},{6,4},{7,5},{8,10},{9,11},{10,... | collective-permute-start | bytes 1032200 | tf_op jit(solution)/shard_map/ppermute | solution.py:105
  152.9 1.3 copy-start.1
  153.1 1.2 copy-start.4

commit v3 on v2

--- a/solution.py
+++ b/solution.py
@@ -9,103 +9,339 @@
 HEADS = 64
 HEAD_DIM = 64
 STATE = 128
-GROUPS = 8
 TOP = 6
-BLOCK_LEN = 256
 
 
 EPSILON = 1e-05
 ROUTE_SCALE = 2.5
-
-
-def shift(x, axis, step):
-    size = lax.axis_size(axis)
-    pairs = [(i, i + step) for i in range(size) if 0 <= i + step < size]
-    return lax.ppermute(x, axis, pairs)
-
-
-def entering(decay, state):
-    count = lax.axis_size("seq") // 2
-    odd = lax.axis_index("seq") % 2 == 1
-    heads, rows, width = state.shape
-
-    def pack(decay, state):
-        tail = jnp.broadcast_to(decay[:, None, None], (heads, 8, width))
-        return jnp.concatenate([state, tail], axis=1).astype(jnp.bfloat16)
-
-    def unpack(packed):
-        wide = packed.astype(jnp.float32)
-        return wide[:, rows, 0], wide[:, :rows]
-
-    def combine(earlier, later):
-        return (earlier[0] * later[0], later[0][:, None, None] * earlier[1] + later[1])
-
-    mine = (decay, state)
-    other = unpack(partner(pack(*mine), "seq", 0))
-    first = jax.tree.map(lambda a, b: jnp.where(odd, a, b), other, mine)
-    second = jax.tree.map(lambda a, b: jnp.where(odd, a, b), mine, other)
-    before = jax.tree.map(lambda a: jnp.where(odd, a, jnp.zeros_like(a)), other)
-    before = (jnp.where(odd, before[0], 1.0), before[1])
-    pair = combine(first, second)
-    reach, scan = 1, unpack(shift(pack(*pair), "seq", 2))
-    while reach < count - 1:
-        scan = combine(unpack(shift(pack(*scan), "seq", 2 * reach)), scan)
-        reach *= 2
-    return combine(scan, before)[1]
-
-
-def gather_columns(block):
-    count = lax.axis_size("seq") // 2
-    place = lax.axis_index("seq") // 2
-    up, down = [block], [block]
-    for step in range(1, count):
-        up.append(shift(up[-1], "seq", 2))
-        down.append(shift(down[-1], "seq", -2))
-    slots = [block]
-    for step in range(1, count):
-        slots.append(jnp.where(place + step < count, down[step], up[count - step]))
-    return [(slot, partner(slot, "seq", 0)) for slot in slots]
-
-
-def project(normed, slots):
-    count = len(slots)
-    place, odd = lax.axis_index("seq") // 2, lax.axis_index("seq") % 2 == 1
-    parts = []
-    for pair in slots:
-        first, second = (
-            jnp.dot(normed, block, preferred_element_type=jnp.float32).astype(jnp.bfloat16)
-            for block in pair
-        )
-        parts.append(
-            jnp.concatenate(
-                [jnp.where(odd, second, first), jnp.where(odd, first, second)], axis=1
-            )
-        )
-    parts = jnp.stack(parts + parts[:-1])
-    parts = lax.dynamic_slice_in_dim(parts, (count - place) % count, count, axis=0)
-    return parts.transpose(1, 0, 2).reshape(normed.shape[0], -1)
-
-
-def sum_rows(x, axis):
-    size = lax.axis_size(axis)
-    bits = size.bit_length() - 1
-    width = x.shape[-1]
-    x = x.reshape((2,) * bits + (-1, width))
-    for bit in range(bits):
-        mine = lax.axis_index(axis) >> bit & 1
-        where = bits - 1 - bit
-        keep = lax.dynamic_index_in_dim(x, mine, where, keepdims=False)
-        give = lax.dynamic_index_in_dim(x, 1 - mine, where, keepdims=False)
-        got = partner(give.astype(jnp.bfloat16), axis, bit)
-        x = keep.astype(jnp.float32) + got.astype(jnp.float32)
-    return x
-
-
-def partner(x, axis, stride):
-    return lax.ppermute(x, axis, [(i, i ^ 1 << stride) for i in range(lax.axis_size(axis))])
-
-
 MESH = pl.DeviceIdType.MESH
+
+
+def mixer_kernel(
+    pairs, heads_mesh, value_ref, gate_ref, write_ref, read_ref, cum_ref, cum_t_ref, step_t_ref,
+    coef_ref, ecum_ref, decay_ref, skip_ref, gain_ref, weight_ref, out_ref,
+    blocks, fresh, y_send, y_got, z_send, z_got, carry, mixed, normed, prod, sums,
+    su, sd, sy, rw, s_state, r_state, ss, rs,
+):
+    seq, head = lax.axis_index("seq"), lax.axis_index("head")
+    z, y = seq // 2, seq % 2
+    mate = {"seq": 2 * z + 1 - y}
+    above, below = {"seq": seq + 2}, {"seq": seq - 2}
+    count = value_ref.shape[0]
+    heads = cum_ref.shape[1]
+    groups = write_ref.shape[1] // STATE
+    per_group = heads // groups
+    lanes = per_group * HEAD_DIM
+    columns = weight_ref.shape[0]
+    pieces = 3 if columns % 48 == 0 else 1
+    piece = columns // pieces
+    own_rows = count // heads_mesh
+    flat = heads * HEAD_DIM
+
+    def remote(src, dst, send, recv, device):
+        return pltpu.make_async_remote_copy(
+            src_ref=src, dst_ref=dst, send_sem=send, recv_sem=recv,
+            device_id=device, device_id_type=MESH,
+        )
+
+    def got(dst, sem):
+        pltpu.make_async_copy(dst, dst, sem).wait()
+
+    barrier = pltpu.get_barrier_semaphore()
+
+    def greet(device):
+        pl.semaphore_signal(barrier, inc=1, device_id=device, device_id_type=MESH)
+
+    greet(mate)
+    for j in range(1, heads_mesh):
+        greet({"head": (head + j) % heads_mesh})
+
+    @pl.when(z < pairs - 1)
+    def _():
+        greet(above)
+
+    @pl.when(z > 0)
+    def _():
+        greet(below)
+
+    blocks[seq] = weight_ref[...]
+    ends = jnp.where(z < pairs - 1, 1, 0) + jnp.where(z > 0, 1, 0)
+    pl.semaphore_wait(barrier, heads_mesh + ends)
+
+    def piece_of(source, i):
+        return blocks.at[source, pl.ds(i * piece, piece)]
+
+    def weight_copy(source, i, sems, device):
+        here = piece_of(source, i)
+        return remote(here, here, sems.at[source, i], rw.at[source, i], device)
+
+    @pl.when(z < pairs - 1)
+    def _():
+        for i in range(pieces):
+            weight_copy(seq, i, su, above).start()
+
+    @pl.when(z > 0)
+    def _():
+        for i in range(pieces):
+            weight_copy(seq, i, sd, below).start()
+
+    low = lax.broadcasted_iota(jnp.int32, (count, 2 * HEAD_DIM), 1) < HEAD_DIM
+
+    def two_heads(ref, h):
+        return jnp.where(low, ref[:, h : h + 1], ref[:, h + 1 : h + 2])
+
+    for h in range(0, heads, 2):
+        g = h // per_group
+        at = slice(h * HEAD_DIM, (h + 2) * HEAD_DIM)
+        weighted = (value_ref[:, at].astype(jnp.float32) * two_heads(coef_ref, h)).astype(
+            jnp.bfloat16
+        )
+        fresh[at, :] = lax.dot_general(
+            weighted, write_ref[:, g * STATE : (g + 1) * STATE], (((0,), (0,)), ((), ())),
+            preferred_element_type=jnp.float32,
+        )
+    y_send[:flat] = fresh[...].astype(jnp.bfloat16)
+    y_send[flat:] = decay_ref[...].astype(jnp.bfloat16)
+    state_y = remote(y_send, y_got, s_state.at[0], r_state.at[0], mate)
+    state_y.start()
+    for i in range(pieces):
+        weight_copy(seq, i, sy, mate).start()
+
+    causal = lax.broadcasted_iota(jnp.int32, (count, count), 0) >= lax.broadcasted_iota(
+        jnp.int32, (count, count), 1
+    )
+
+    def inner(g):
+        where = slice(g * STATE, (g + 1) * STATE)
+        scores = lax.dot_general(
+            read_ref[:, where], write_ref[:, where], (((1,), (1,)), ((), ())),
+            preferred_element_type=jnp.float32,
+        )
+        for h in range(g * per_group, (g + 1) * per_group, 2):
+            at = slice(h * HEAD_DIM, (h + 2) * HEAD_DIM)
+            sides = []
+            for n in (h, h + 1):
+                decays = jnp.exp(
+                    jnp.where(causal, cum_ref[:, n : n + 1] - cum_t_ref[n : n + 1, :], 0.0)
+                )
+                mixing = jnp.where(causal, scores * decays * step_t_ref[n : n + 1, :], 0.0)
+                sides.append(
+                    jnp.dot(
+                        mixing.astype(jnp.bfloat16), value_ref[:, at],
+                        preferred_element_type=jnp.float32,
+                    )
+                )
+            mixed[:, at] = jnp.where(low, sides[0], sides[1]) + skip_ref[
+                :, at
+            ] * value_ref[:, at].astype(jnp.float32)
+
+    def spread(decay):
+        wide = jnp.broadcast_to(decay[:heads, None, :], (heads, HEAD_DIM, STATE))
+        return wide.reshape(flat, STATE)
+
+    def relay(k):
+        for valid, onward, source, sems, device in (
+            (z >= k, z < pairs - 1, seq - 2 * k, su, above),
+            (z + k < pairs, z > 0, seq + 2 * k, sd, below),
+        ):
+
+            @pl.when(valid)
+            def _(onward=onward, source=source, sems=sems, device=device):
+                for i in range(pieces):
+                    got(piece_of(source, i), rw.at[source, i])
+
+                    @pl.when(onward)
+                    def _():
+                        weight_copy(source, i, sems, device).start()
+
+                    weight_copy(source, i, sy, mate).start()
+
+    inner(0)
+    state_y.wait()
+    theirs = y_got[:flat].astype(jnp.float32)
+    their_decay = spread(y_got[flat:].astype(jnp.float32))
+    my_decay = spread(decay_ref[...])
+    pair_state = jnp.where(
+        y == 1, my_decay * theirs + fresh[...], their_decay * fresh[...] + theirs
+    )
+    state_z = remote(z_send, z_got, s_state.at[1], r_state.at[1], above)
+
+    @pl.when(z == 0)
+    def _():
+        z_send[...] = pair_state.astype(jnp.bfloat16)
+        z_got[...] = jnp.zeros_like(z_got)
+        state_z.start()
+
+    for g in range(1, groups):
+        inner(g)
+    relay(1)
+
+    @pl.when(z > 0)
+    def _():
+        got(z_got, r_state.at[1])
+
+        @pl.when(z < pairs - 1)
+        def _():
+            z_send[...] = (
+                my_decay * their_decay * z_got[...].astype(jnp.float32) + pair_state
+            ).astype(jnp.bfloat16)
+            state_z.start()
+
+    entered = z_got[...].astype(jnp.float32)
+    carry[...] = jnp.where(y == 1, their_decay * entered + theirs, entered).astype(jnp.bfloat16)
+    for g in range(groups):
+        at = slice(g * lanes, (g + 1) * lanes)
+        carried = lax.dot_general(
+            read_ref[:, g * STATE : (g + 1) * STATE], carry[at, :], (((1,), (1,)), ((), ())),
+            preferred_element_type=jnp.float32,
+        )
+        scale = jnp.concatenate(
+            [two_heads(ecum_ref, h) for h in range(g * per_group, (g + 1) * per_group, 2)], axis=1
+        )
+        gate = gate_ref[:, at].astype(jnp.float32)
+        gated = (mixed[:, at] + carried * scale) * (gate * jax.nn.sigmoid(gate))
+        inv_rms = lax.rsqrt(jnp.mean(gated * gated, axis=-1, keepdims=True) + EPSILON)
+        normed[:, at] = (gated * inv_rms * gain_ref[:, at]).astype(jnp.bfloat16)
+
+    def chunk_of(source, to):
+        rows = pl.ds(pl.multiple_of(to * own_rows, own_rows), own_rows)
+        return prod.at[source, rows]
+
+    def give(source, to):
+        return remote(
+            chunk_of(source, to), sums.at[source, head], ss.at[source, to], rs.at[source, head],
+            {"head": to},
+        )
+
+    def project(source):
+        prod[source, :, pl.ds(0, columns)] = lax.dot_general(
+            normed[...], blocks[source], (((1,), (1,)), ((), ())),
+            preferred_element_type=jnp.float32,
+        ).astype(jnp.bfloat16)
+        for j in range(1, heads_mesh):
+            give(source, (head + j) % heads_mesh).start()
+
+    def arrived(source):
+        for i in range(pieces):
+            got(piece_of(source, i), rw.at[source, i])
+
+    across = 1 - 2 * y
+    prod[...] = jnp.zeros_like(prod)
+    project(seq)
+    for k in range(1, pairs):
+        if k > 1:
+            relay(k)
+        if k == 1:
+            arrived(seq + across)
+            project(seq + across)
+        for valid, source in ((z >= k, seq - 2 * k), (z + k < pairs, seq + 2 * k)):
+
+            @pl.when(valid)
+            def _(source=source):
+                project(source)
+
+        for valid, source in ((z >= k, seq - 2 * k), (z + k < pairs, seq + 2 * k)):
+
+            @pl.when(valid)
+            def _(source=source):
+                arrived(source + across)
+                project(source + across)
+
+    def collect(source, carry_on):
+        rows = pl.ds(pl.multiple_of(head * own_rows, own_rows), own_rows)
+        total = prod[source, rows].astype(jnp.float32)
+        for j in range(1, heads_mesh):
+            other = (head + j) % heads_mesh
+            got(sums.at[source, other], rs.at[source, other])
+            total += sums[source, other].astype(jnp.float32)
+        out_ref[source] = total
+        return carry_on
+
+    lax.fori_loop(0, 2 * pairs, collect, 0)
+
+    @pl.when(z < pairs - 1)
+    def _():
+        state_z.wait_send()
+        for i in range(pieces):
+            weight_copy(seq, i, su, above).wait_send()
+
+    @pl.when(z > 0)
+    def _():
+        for i in range(pieces):
+            weight_copy(seq, i, sd, below).wait_send()
+
+    for k in range(pairs):
+        for valid, onward, source, sems, device in (
+            (z >= k, z < pairs - 1, seq - 2 * k, su, above),
+            (z + k < pairs, z > 0, seq + 2 * k, sd, below),
+        ):
+            if k == 0 and sems is sd:
+                continue
+
+            @pl.when(valid)
+            def _(k=k, onward=onward, source=source, sems=sems, device=device):
+                for i in range(pieces):
+                    weight_copy(source, i, sy, mate).wait_send()
+                    if k > 0:
+
+                        @pl.when(onward)
+                        def _():
+                            weight_copy(source, i, sems, device).wait_send()
+
+    def sent(source, carry_on):
+        for j in range(1, heads_mesh):
+            give(source, (head + j) % heads_mesh).wait_send()
+        return carry_on
+
+    lax.fori_loop(0, 2 * pairs, sent, 0)
+
+
+def mixer(values, gates, writes, reads, cumulative, steps, skip_gain, norm_gain, weight):
+    count, heads = cumulative.shape
+    pairs, heads_mesh = lax.axis_size("seq") // 2, lax.axis_size("head")
+    total = cumulative[-1:]
+    coef = jnp.exp(total - cumulative) * steps
+    decay = jnp.zeros((16, STATE), jnp.float32).at[:heads].set(
+        jnp.broadcast_to(jnp.exp(total).T, (heads, STATE))
+    )
+    turned = weight.T
+    columns, rows = turned.shape
+    flat = heads * HEAD_DIM
+    padded = -(-columns // 128) * 128
+    pieces = 3 if columns % 48 == 0 else 1
+    size = 2 * pairs
+    dma = pltpu.SemaphoreType.DMA
+    bf16 = jnp.bfloat16
+    vmem = pl.BlockSpec(memory_space=pltpu.VMEM)
+    out = pl.pallas_call(
+        functools.partial(mixer_kernel, pairs, heads_mesh),
+        out_shape=jax.ShapeDtypeStruct((size, count // heads_mesh, padded), jnp.float32),
+        in_specs=[vmem] * 13,
+        out_specs=vmem,
+        scratch_shapes=[
+            pltpu.VMEM((size, columns, rows), bf16),
+            pltpu.VMEM((flat, STATE), jnp.float32),
+            pltpu.VMEM((flat + 16, STATE), bf16),
+            pltpu.VMEM((flat + 16, STATE), bf16),
+            pltpu.VMEM((flat, STATE), bf16),
+            pltpu.VMEM((flat, STATE), bf16),
+            pltpu.VMEM((flat, STATE), bf16),
+            pltpu.VMEM((count, flat), jnp.float32),
+            pltpu.VMEM((count, flat), bf16),
+            pltpu.VMEM((size, count, padded), bf16),
+            pltpu.VMEM((size, heads_mesh, count // heads_mesh, padded), bf16),
+            dma((size, pieces)), dma((size, pieces)), dma((size, pieces)), dma((size, pieces)),
+            dma((2,)), dma((2,)),
+            dma((size, heads_mesh)), dma((size, heads_mesh)),
+        ],
+        compiler_params=pltpu.CompilerParams(
+            collective_id=0, has_side_effects=True, vmem_limit_bytes=48 * 1024 * 1024
+        ),
+    )(
+        values, gates, writes, reads, cumulative, cumulative.T, steps.T, coef,
+        jnp.exp(cumulative), decay, jnp.repeat(skip_gain, HEAD_DIM)[None], norm_gain[None], turned,
+    )
+    return out[:, :, :columns].transpose(1, 0, 2).reshape(count // heads_mesh, size * columns)
 
 
 def moe_kernel(
@@ -236,7 +472,9 @@
         def gather_up(i, carry):
             at = pl.ds(pl.multiple_of(i * deep, 128), deep)
             taken = rows[block, :, :, at].reshape(2 * slots, deep)
-            total[...] += jnp.dot(taken, up[at, :], preferred_element_type=jnp.float32)
+            total[...] += lax.dot_general(
+                taken, up[:, at], (((1,), (1,)), ((), ())), preferred_element_type=jnp.float32
+            )
             return carry
 
         lax.fori_loop(0, width // deep, gather_up, 0)
@@ -326,7 +564,7 @@
         in_specs=[vmem, vmem, vmem, pl.BlockSpec(memory_space=pl.ANY), pl.BlockSpec(memory_space=pl.ANY)],
         out_specs=vmem,
         scratch_shapes=[
-            pltpu.VMEM((width, units), bf16),
+            pltpu.VMEM((units, width), bf16),
             pltpu.VMEM((units, width), bf16),
             pltpu.VMEM((planes, count, width), bf16),
             pltpu.VMEM((planes, 2 * count, slots), bf16),
@@ -355,7 +593,7 @@
             bytes_accessed=4 * width * units,
             transcendentals=0,
         ),
-    )(inputs, info, hidden, up_weight, down_weight)
+    )(inputs, info, hidden, up_weight.swapaxes(1, 2), down_weight)
 
 
 def per_device(
@@ -375,87 +613,14 @@
     up_weight,
     down_weight,
 ):
-    slots = gather_columns(out_weight)
     tokens_dev = ssm_values.shape[0]
-    heads_dev = step_size.shape[1]
-    per_group = HEADS // GROUPS
-    groups_dev = heads_dev // per_group
-    count_blocks = tokens_dev // BLOCK_LEN
     decay_rates = jnp.exp2(-decay_power.astype(jnp.float32))
-    values = ssm_values.reshape(count_blocks, BLOCK_LEN, heads_dev, HEAD_DIM)
-    steps_all = step_size.reshape(count_blocks, BLOCK_LEN, heads_dev)
-    writes = write_proj.reshape(count_blocks, BLOCK_LEN, groups_dev, STATE)
-    reads = read_proj.reshape(count_blocks, BLOCK_LEN, groups_dev, STATE)
-    causal = jnp.tril(jnp.ones((BLOCK_LEN, BLOCK_LEN), dtype=bool))
-
-    def one_block(pieces):
-        values_in, steps_in, write_in, read_in = pieces
-        log_decay = -steps_in * decay_rates[None, :]
-        cumulative = jnp.cumsum(log_decay, axis=0)
-        scores = jnp.einsum("tgn,sgn->gts", read_in, write_in, preferred_element_type=jnp.float32)
-        scores = jnp.repeat(scores, per_group, axis=0)
-        decays = jnp.exp(cumulative.T[:, :, None] - cumulative.T[:, None, :])
-        mixing = jnp.where(causal[None], scores * decays * steps_in.T[:, None, :], 0.0).astype(
-            jnp.bfloat16
-        )
-        inner_out = jnp.einsum(
-            "hts,shp->thp", mixing, values_in, preferred_element_type=jnp.float32
-        )
-        block_total = cumulative[-1]
-        weighted = (
-            values_in.astype(jnp.float32)
-            * (jnp.exp(block_total[None, :] - cumulative) * steps_in)[:, :, None]
-        ).astype(jnp.bfloat16)
-        write_heads = jnp.repeat(write_in, per_group, axis=1)
-        fresh_state = jnp.einsum(
-            "shp,shn->hpn", weighted, write_heads, preferred_element_type=jnp.float32
-        )
-        return (inner_out, fresh_state, block_total, cumulative)
-
-    inner_all, fresh_all, totals_blk, cumul_all = lax.map(
-        one_block, (values, steps_all, writes, reads)
+    cumulative = jnp.cumsum(-step_size * decay_rates[None, :], axis=0)
+    mixed_out = mixer(
+        ssm_values, ssm_gate, write_proj, read_proj, cumulative, step_size, skip_gain, norm_gain,
+        out_weight,
     )
-
-    def summarize(carried_in, pieces):
-        decay_prod, summary = carried_in
-        block_total, fresh_state = pieces
-        factor = jnp.exp(block_total)
-        return ((decay_prod * factor, factor[:, None, None] * summary + fresh_state), None)
-
-    zero_state = jnp.zeros((heads_dev, HEAD_DIM, STATE), jnp.float32)
-    (device_decay, device_state), unused = lax.scan(
-        summarize, (jnp.ones((heads_dev,), jnp.float32), zero_state), (totals_blk, fresh_all)
-    )
-
-    incoming = entering(device_decay, device_state)
-
-    def emit_rows(carry_state, pieces):
-        read_in, cumulative, block_total, fresh_state = pieces
-        read_heads = jnp.repeat(read_in, per_group, axis=1)
-        carried = jnp.einsum(
-            "thn,hpn->thp",
-            read_heads,
-            carry_state.astype(jnp.bfloat16),
-            preferred_element_type=jnp.float32,
-        )
-        carried = carried * jnp.exp(cumulative)[:, :, None]
-        return (jnp.exp(block_total)[:, None, None] * carry_state + fresh_state, carried)
-
-    final_state, carried_all = lax.scan(
-        emit_rows, incoming, (reads, cumul_all, totals_blk, fresh_all)
-    )
-    values_flat = ssm_values.reshape(tokens_dev, heads_dev, HEAD_DIM).astype(jnp.float32)
-    ssm_out = (inner_all + carried_all).reshape(tokens_dev, heads_dev, HEAD_DIM) + skip_gain[
-        None, :, None
-    ] * values_flat
-    gate_vals = ssm_gate.reshape(tokens_dev, heads_dev, HEAD_DIM).astype(jnp.float32)
-    gated = (ssm_out * jax.nn.silu(gate_vals)).reshape(tokens_dev, groups_dev, per_group * HEAD_DIM)
-    inv_rms = lax.rsqrt(jnp.mean(gated * gated, axis=-1, keepdims=True) + EPSILON)
-    normed = (
-        (gated * inv_rms).reshape(tokens_dev, heads_dev * HEAD_DIM) * norm_gain[None, :]
-    ).astype(jnp.bfloat16)
     rows_own = tokens_dev // lax.axis_size("head")
-    mixed_out = sum_rows(project(normed, slots), "head")
     hidden = residual.astype(jnp.float32) + mixed_out
     inputs = (
         hidden

time: 257 us -> 203 us (0.79)
  Pallas kernels: 99.8 us -> 185 us
  waiting for transfers between devices: 70.8 us -> 0 us
  starting transfers between devices: 45.3 us -> 0 us
  matrix products: 8.49 us -> 0.18 us
  local copies, waits for them, and re-layouts: 19.5 us -> 11.8 us
  other arithmetic: 11.1 us -> 4.71 us
    pallas_call x0 -> x1, Pallas kernels: none -> 84.8 us  [mixer(): pl.pallas_call(functools.partial(mixer_kernel, pairs, heads_mesh), out_sh...]
    ppermute x16 -> x0, waiting for transfers between devices: 70.8 us -> none  [the longest x7 44.4 us: partner(): lax.ppermute(x, axis, [(i, i ^ 1 << stride) for i in range(lax.axis_size(...]
    ppermute x16 -> x0, starting transfers between devices: 45.3 us -> none  [the longest x9 34.4 us: shift(): return lax.ppermute(x, axis, pairs)]
    dot_general x12 -> x0, matrix products: 8.32 us -> none  [the longest x8 5.26 us: project(): jnp.dot(normed, block, preferred_element_type=jnp.float32)]
    select_n x4 -> x0, other arithmetic: 2.66 us -> none  [the longest x3 2.46 us: gather_columns(): slots.append(jnp.where(place + step < count, down[step], up[count - step]))]
    unnamed x33 -> x29, local copies, waits for them, and re-layouts: 11.4 us -> 9.07 us
  transfers between devices with their start and end apart: 16 -> 0, of which waited for: 9 -> 0; matrix products, arithmetic and copies ran while one was open for 10% -> 0% of each run, Pallas kernels for 0% -> 0%
where the time goes in v3:
time: 203 us; the launch traced here: 202 us
  Pallas kernels  185 us (91%)
  local copies, waits for them, and re-layouts  11.8 us (6%)
  other arithmetic  4.71 us (2%)
    pallas_call x1, Pallas kernels, expert_layer(): pl.pallas_call(functools.partial(moe_kernel, planes, cols, cap), out_shap...  100 us
    pallas_call x1, Pallas kernels, mixer(): pl.pallas_call(functools.partial(mixer_kernel, pairs, heads_mesh), out_sh...  84.8 us
    unnamed x29, local copies, waits for them, and re-layouts  9.07 us

profile of v3, /device:TPU:0, one launch (start us, length us, event | category | flops | bytes accessed | tf_op | source)
XLA Modules:
  0.0 202.1 jit_solution(116526014662055635)
XLA Ops:
  0.0 0.0 copy-start
  0.0 0.7 multiply_exponential_fusion
  0.7 0.8 copy_bitcast_fusion.2
  1.5 0.6 reduce-window.14
  2.1 0.2 slice_reduce_fusion.1
  2.3 0.1 broadcast_add_fusion
  2.4 0.1 copy.52
  2.5 0.8 copy.54
  3.4 0.0 copy-start.12
  3.4 0.1 scatter.4.decay_ref
  3.4 0.1 copy.55.cum_t_ref
  3.5 0.7 broadcast_in_dim.27
  4.2 0.1 broadcast_in_dim_reshape.3.skip_ref
  4.3 1.1 copy-done.1
  5.4 1.0 copy-done.2
  6.5 1.0 copy-done.3
  7.5 0.7 copy-done.4
  8.2 0.9 copy-done.5
  9.1 0.9 copy-done.6
  10.0 0.7 copy-done.7
  10.7 84.8 %shard_map.150 = f32[8,64,384]{2,1,0:T(8,128)S(1)} custom-call(bf16[256,1024]{1,0:T(8,128)(2,1)S(1)} %copy-done.2, bf16[256,1024]{1,0:T(8,128)(2,1)S(1)} %copy-done.3, bf16[256,256]{1,0:T(8,128)(2,1)S(1)} %copy-done.5, bf16[256,256]{1,0:T(8,128)(2,1)S(1)} %copy-done.6, f32[256,16]{1,0:T(8,128)S(1)} %bitcast.59, f32[16,256]{1,0:T(8,128)S(1)} %copy.55.cum_t_ref, ...), custom_call_target="tpu_custom_call" | custom-call | tf_op jit(solution)/shard_map/pallas_call | solution.py:316
  95.5 0.1 slice_bitcast_fusion
  95.6 0.5 copy.56
  96.1 0.3 reshape.104
  96.3 0.0 copy-done.10
  96.3 0.2 multiply_reduce_fusion
  96.6 0.0 copy-done.12
  96.6 0.1 multiply_convert_fusion.x_ref
  96.7 0.0 copy-done
  96.7 0.0 copy-start.9
  96.7 0.2 fusion.6
  96.9 0.0 copy-done.11
  96.9 0.1 select_reduce_fusion.1
  97.0 0.1 copy.57
  97.1 0.2 eq.49
  97.3 0.9 reduce-window.16
  98.1 0.2 slice_reduce_fusion
  98.4 0.1 eq.45
  98.5 0.1 fusion.3
  98.6 0.1 reshape.106
  98.8 0.1 copy.60
  98.9 0.2 select_reduce_fusion
  99.1 0.2 fusion
  99.3 0.7 maximum_bitcast_fusion.info_ref
  99.9 0.0 copy-done.8
  99.9 0.0 copy-done.9
  99.9 100.5 %shard_map.151 = bf16[64,2688]{1,0:T(8,128)(2,1)} custom-call(bf16[64,2688]{1,0:T(8,128)(2,1)} %copy-done.9, bf16[4,128,128]{2,1,0:T(8,128)(2,1)} %maximum_bitcast_fusion.info_ref, f32[64,2688]{1,0:T(8,128)} %copy-done.8, bf16[1,928,2688]{2,1,0:T(8,128)(2,1)} %bitcast.64, bf16[1,928,2688]{2,1,0:T(8,128)(2,1)} %down_hbm.1), custom_call_target="tpu_custom_call" | custom-call | flops 10217324544 | bytes 9977856 | tf_op jit(solution)/shard_map/pallas_call | solution.py:561
  200.4 1.7 copy.72
  (21 shorter events, 0.2 us)
Async XLA Ops:
  0.0 96.7 %copy-start = (bf16[2688,16]{0,1:T(8,128)(2,1)S(1)}, bf16[2688,16]{0,1:T(8,128)(2,1)}, u32[]{:S(2)}) copy-start(bf16[2688,16]{0,1:T(8,128)(2,1)} %param.30) | copy-start | bytes 258052
  0.0 96.3 %copy-start.10 = (bf16[64,2688]{1,0:T(8,128)(2,1)S(1)}, bf16[64,2688]{1,0:T(8,128)(2,1)}, u32[]{:S(2)}) copy-start(bf16[64,2688]{1,0:T(8,128)(2,1)} %param.28) | copy-start | bytes 1032196
  3.4 93.2 %copy-start.12 = (f32[2688]{0:T(1024)S(1)}, f32[2688]{0:T(1024)}, u32[]{:S(2)}) copy-start(f32[2688]{0:T(1024)} %param.29) | copy-start | bytes 32260
  4.3 1.1 copy-start.1
  5.4 1.0 copy-start.2
  6.5 1.0 copy-start.3
  7.5 0.7 copy-start.4
  8.2 0.9 copy-start.5
  9.1 0.9 copy-start.6
  10.0 0.7 copy-start.7
  10.7 86.2 %copy-start.11 = (s32[64,6]{0,1:T(8,128)S(1)}, s32[64,6]{0,1:T(8,128)}, u32[]{:S(2)}) copy-start(s32[64,6]{0,1:T(8,128)} %param.31) | copy-start | bytes 4612
  96.5 3.4 %copy-start.8 = (f32[64,2688]{1,0:T(8,128)}, f32[64,2688]{1,0:T(8,128)S(1)}, u32[]{:S(2)}) copy-start(f32[64,2688]{1,0:T(8,128)S(1)} %get-tuple-element.26.hidden_ref) | copy-start | bytes 2064388
  96.7 3.2 %copy-start.9 = (bf16[64,2688]{1,0:T(8,128)(2,1)}, bf16[64,2688]{1,0:T(8,128)(2,1)S(1)}, u32[]{:S(2)}) copy-start(bf16[64,2688]{1,0:T(8,128)(2,1)S(1)} %multiply_convert_fusion.x_ref) | copy-start | bytes 1032196

commit v4 on v3

--- a/solution.py
+++ b/solution.py
@@ -18,21 +18,21 @@
 
 
 def mixer_kernel(
-    pairs, heads_mesh, value_ref, gate_ref, write_ref, read_ref, cum_ref, cum_t_ref, step_t_ref,
-    coef_ref, ecum_ref, decay_ref, skip_ref, gain_ref, weight_ref, out_ref,
+    pairs, heads_mesh, value_hbm, gate_hbm, write_hbm, read_hbm, step_t_ref, rate_ref, skip_ref,
+    gain_ref, weight_hbm, out_ref,
+    value_ref, gate_ref, write_ref, read_ref, cum_ref, cum_t_ref, coef_ref, ecum_ref, decay_ref,
     blocks, fresh, y_send, y_got, z_send, z_got, carry, mixed, normed, prod, sums,
-    su, sd, sy, rw, s_state, r_state, ss, rs,
+    loads, su, sd, sy, rw, s_state, r_state, ss, rs,
 ):
     seq, head = lax.axis_index("seq"), lax.axis_index("head")
     z, y = seq // 2, seq % 2
     mate = {"seq": 2 * z + 1 - y}
     above, below = {"seq": seq + 2}, {"seq": seq - 2}
-    count = value_ref.shape[0]
-    heads = cum_ref.shape[1]
-    groups = write_ref.shape[1] // STATE
+    heads, count = step_t_ref.shape
+    groups = write_hbm.shape[1] // STATE
     per_group = heads // groups
     lanes = per_group * HEAD_DIM
-    columns = weight_ref.shape[0]
+    columns = weight_hbm.shape[0]
     pieces = 3 if columns % 48 == 0 else 1
     piece = columns // pieces
     own_rows = count // heads_mesh
@@ -64,7 +64,17 @@
     def _():
         greet(below)
 
-    blocks[seq] = weight_ref[...]
+    copies = [
+        pltpu.make_async_copy(there, here, loads.at[i])
+        for i, (there, here) in enumerate(
+            (
+                (value_hbm, value_ref), (write_hbm, write_ref), (read_hbm, read_ref),
+                (gate_hbm, gate_ref), (weight_hbm, blocks.at[seq]),
+            )
+        )
+    ]
+    for copy in copies:
+        copy.start()
     ends = jnp.where(z < pairs - 1, 1, 0) + jnp.where(z > 0, 1, 0)
     pl.semaphore_wait(barrier, heads_mesh + ends)
 
@@ -75,15 +85,49 @@
         here = piece_of(source, i)
         return remote(here, here, sems.at[source, i], rw.at[source, i], device)
 
+    def own_copy(i, sems, device):
+        return remote(
+            weight_hbm.at[pl.ds(i * piece, piece)], piece_of(seq, i), sems.at[seq, i],
+            rw.at[seq, i], device,
+        )
+
     @pl.when(z < pairs - 1)
     def _():
         for i in range(pieces):
-            weight_copy(seq, i, su, above).start()
+            own_copy(i, su, above).start()
 
     @pl.when(z > 0)
     def _():
         for i in range(pieces):
-            weight_copy(seq, i, sd, below).start()
+            own_copy(i, sd, below).start()
+
+    causal = lax.broadcasted_iota(jnp.int32, (count, count), 0) >= lax.broadcasted_iota(
+        jnp.int32, (count, count), 1
+    )
+    diagonal = lax.broadcasted_iota(jnp.int32, (count, count), 0) == lax.broadcasted_iota(
+        jnp.int32, (count, count), 1
+    )
+
+    def sums_of(a, b):
+        return lax.dot_general(
+            a, b, (((1,), (1,)), ((), ())), precision=lax.Precision.HIGHEST,
+            preferred_element_type=jnp.float32,
+        )
+
+    triangle = jnp.where(causal, 1.0, 0.0)
+    log_decay = -step_t_ref[...] * rate_ref[...]
+    cumulative = sums_of(triangle, log_decay)
+    steps = sums_of(jnp.where(diagonal, 1.0, 0.0), step_t_ref[...])
+    cum_ref[...] = cumulative
+    cum_t_ref[...] = sums_of(log_decay, triangle)
+    coef_ref[...] = jnp.exp(cumulative[count - 1 :] - cumulative) * steps
+    ecum_ref[...] = jnp.exp(cumulative)
+    decay_ref[...] = jnp.zeros_like(decay_ref)
+    decay_ref[:heads] = jnp.broadcast_to(
+        jnp.exp(cum_t_ref[:, count - 1 : count]), (heads, STATE)
+    )
+    copies[0].wait()
+    copies[1].wait()
 
     low = lax.broadcasted_iota(jnp.int32, (count, 2 * HEAD_DIM), 1) < HEAD_DIM
 
@@ -105,11 +149,8 @@
     state_y = remote(y_send, y_got, s_state.at[0], r_state.at[0], mate)
     state_y.start()
     for i in range(pieces):
-        weight_copy(seq, i, sy, mate).start()
-
-    causal = lax.broadcasted_iota(jnp.int32, (count, count), 0) >= lax.broadcasted_iota(
-        jnp.int32, (count, count), 1
-    )
+        own_copy(i, sy, mate).start()
+    copies[2].wait()
 
     def inner(g):
         where = slice(g * STATE, (g + 1) * STATE)
@@ -189,6 +230,7 @@
 
     entered = z_got[...].astype(jnp.float32)
     carry[...] = jnp.where(y == 1, their_decay * entered + theirs, entered).astype(jnp.bfloat16)
+    copies[3].wait()
     for g in range(groups):
         at = slice(g * lanes, (g + 1) * lanes)
         carried = lax.dot_general(
@@ -227,6 +269,7 @@
 
     across = 1 - 2 * y
     prod[...] = jnp.zeros_like(prod)
+    copies[4].wait()
     project(seq)
     for k in range(1, pairs):
         if k > 1:
@@ -263,12 +306,12 @@
     def _():
         state_z.wait_send()
         for i in range(pieces):
-            weight_copy(seq, i, su, above).wait_send()
+            own_copy(i, su, above).wait_send()
 
     @pl.when(z > 0)
     def _():
         for i in range(pieces):
-            weight_copy(seq, i, sd, below).wait_send()
+            own_copy(i, sd, below).wait_send()
 
     for k in range(pairs):
         for valid, onward, source, sems, device in (
@@ -281,8 +324,10 @@
             @pl.when(valid)
             def _(k=k, onward=onward, source=source, sems=sems, device=device):
                 for i in range(pieces):
-                    weight_copy(source, i, sy, mate).wait_send()
-                    if k > 0:
+                    if k == 0:
+                        own_copy(i, sy, mate).wait_send()
+                    else:
+                        weight_copy(source, i, sy, mate).wait_send()
 
                         @pl.when(onward)
                         def _():
@@ -296,14 +341,9 @@
     lax.fori_loop(0, 2 * pairs, sent, 0)
 
 
-def mixer(values, gates, writes, reads, cumulative, steps, skip_gain, norm_gain, weight):
-    count, heads = cumulative.shape
+def mixer(values, gates, writes, reads, steps, rates, skip_gain, norm_gain, weight):
+    count, heads = steps.shape
     pairs, heads_mesh = lax.axis_size("seq") // 2, lax.axis_size("head")
-    total = cumulative[-1:]
-    coef = jnp.exp(total - cumulative) * steps
-    decay = jnp.zeros((16, STATE), jnp.float32).at[:heads].set(
-        jnp.broadcast_to(jnp.exp(total).T, (heads, STATE))
-    )
     turned = weight.T
     columns, rows = turned.shape
     flat = heads * HEAD_DIM
@@ -313,12 +353,22 @@
     dma = pltpu.SemaphoreType.DMA
     bf16 = jnp.bfloat16
     vmem = pl.BlockSpec(memory_space=pltpu.VMEM)
+    anywhere = pl.BlockSpec(memory_space=pl.ANY)
     out = pl.pallas_call(
         functools.partial(mixer_kernel, pairs, heads_mesh),
         out_shape=jax.ShapeDtypeStruct((size, count // heads_mesh, padded), jnp.float32),
-        in_specs=[vmem] * 13,
+        in_specs=[anywhere] * 4 + [vmem] * 4 + [anywhere],
         out_specs=vmem,
         scratch_shapes=[
+            pltpu.VMEM(values.shape, bf16),
+            pltpu.VMEM(gates.shape, bf16),
+            pltpu.VMEM(writes.shape, bf16),
+            pltpu.VMEM(reads.shape, bf16),
+            pltpu.VMEM((count, heads), jnp.float32),
+            pltpu.VMEM((heads, count), jnp.float32),
+            pltpu.VMEM((count, heads), jnp.float32),
+            pltpu.VMEM((count, heads), jnp.float32),
+            pltpu.VMEM((16, STATE), jnp.float32),
             pltpu.VMEM((size, columns, rows), bf16),
             pltpu.VMEM((flat, STATE), jnp.float32),
             pltpu.VMEM((flat + 16, STATE), bf16),
@@ -330,6 +380,7 @@
             pltpu.VMEM((count, flat), bf16),
             pltpu.VMEM((size, count, padded), bf16),
             pltpu.VMEM((size, heads_mesh, count // heads_mesh, padded), bf16),
+            dma((5,)),
             dma((size, pieces)), dma((size, pieces)), dma((size, pieces)), dma((size, pieces)),
             dma((2,)), dma((2,)),
             dma((size, heads_mesh)), dma((size, heads_mesh)),
@@ -338,8 +389,8 @@
             collective_id=0, has_side_effects=True, vmem_limit_bytes=48 * 1024 * 1024
         ),
     )(
-        values, gates, writes, reads, cumulative, cumulative.T, steps.T, coef,
-        jnp.exp(cumulative), decay, jnp.repeat(skip_gain, HEAD_DIM)[None], norm_gain[None], turned,
+        values, gates, writes, reads, steps.T, rates[:, None],
+        jnp.repeat(skip_gain, HEAD_DIM)[None], norm_gain[None], turned,
     )
     return out[:, :, :columns].transpose(1, 0, 2).reshape(count // heads_mesh, size * columns)
 
@@ -347,7 +398,7 @@
 def moe_kernel(
     planes, cols, cap, x_ref, info_ref, hidden_ref, up_hbm, down_hbm, out_ref,
     up, down, xz, iz, pk, rows, act, own, other, back, rb, pt, fin, total,
-    weight_sem, sx, rx, si, ri, sp, rp, sf, rf, sb, rbk, sr, rr, sn, rn,
+    weight_sem, sx_up, sx_down, rx, si, ri, sp, rp, sf, rf, sb, rbk, sr, rr, sn, rn,
 ):
     seq, head = lax.axis_index("seq"), lax.axis_index("head")
     wide = cols // 2
@@ -372,6 +423,7 @@
             device_id=device, device_id_type=MESH,
         )
 
+    xz[z] = x_ref[...]
     load_up = pltpu.make_async_copy(up_hbm.at[0], up, weight_sem.at[0])
     load_down = pltpu.make_async_copy(down_hbm.at[0], down, weight_sem.at[1])
     load_up.start()
@@ -389,8 +441,8 @@
     pl.semaphore_signal(barrier, inc=1, device_id=mate, device_id_type=MESH)
     pl.semaphore_wait(barrier, planes + cols - 1)
 
-    def line_rows(to):
-        return remote(x_ref, xz.at[z], sx.at[to], rx.at[z], in_line(to))
+    def line_rows(block, sems, to):
+        return remote(xz.at[block], xz.at[block], sems.at[block], rx.at[block], in_line(to))
 
     def line_info(to):
         return remote(info_ref.at[to], iz.at[z], si.at[to], ri.at[z], in_line(to))
@@ -423,23 +475,38 @@
     def got(dst, sem):
         pltpu.make_async_copy(dst, dst, sem).wait()
 
+    def source(d):
+        near = jnp.minimum(z, planes - 1 - z)
+        sign = jnp.where(d % 2 == 1, -1, 1)
+        far = jnp.where(z == near, z + (d - near), z - (d - near))
+        return jnp.where(d <= 2 * near, z + sign * ((d + 1) // 2), far)
+
+    def onward(block, act):
+        @pl.when((block <= z) & (z < planes - 1))
+        def _():
+            act(line_rows(block, sx_up, z + 1))
+
+        @pl.when((block >= z) & (z > 0))
+        def _():
+            act(line_rows(block, sx_down, z - 1))
+
+    onward(z, lambda copy: copy.start())
     for d in range(1, planes):
-        line_rows((z + d) % planes).start()
         line_info((z + d) % planes).start()
 
     mine = pl.ds(pl.multiple_of(k * cap, cap), cap)
 
     def pack(d):
-        block = (z + planes - d) % planes
+        block = source(d)
 
         @pl.when(d == 0)
         def _():
-            xz[z] = x_ref[...]
             iz[z] = info_ref[z]
 
         @pl.when(d > 0)
         def _():
             got(xz.at[block], rx.at[block])
+            onward(block, lambda copy: copy.start())
             got(iz.at[block], ri.at[block])
 
         pk[block] = lax.dot_general(
@@ -451,7 +518,7 @@
         rows[block, 0, mine] = pk[block, mine]
 
     def pass_on(d):
-        block = (z + planes - d) % planes
+        block = source(d)
         for j in range(1, cols):
             col = (k + j) % cols
             place = pl.ds(pl.multiple_of(col * cap, cap), cap)
@@ -459,7 +526,7 @@
         forward(block).start()
 
     def compute(d):
-        block = (z + planes - d) % planes
+        block = source(d)
 
         @pl.when(d == 0)
         def _():
@@ -493,7 +560,7 @@
         half_back(block).start()
 
     def add_halves(d):
-        block = (z + planes - d) % planes
+        block = source(d)
         got(back.at[block], rbk.at[block])
         own[block] = (
             own[block].astype(jnp.float32) + back[block].astype(jnp.float32)
@@ -503,7 +570,7 @@
         rb[block, mine] = own[block, mine]
 
     def combine(d):
-        block = (z + planes - d) % planes
+        block = source(d)
         for j in range(1, cols):
             col = (k + j) % cols
             place = pl.ds(pl.multiple_of(col * cap, cap), cap)
@@ -517,7 +584,7 @@
             line_back(block).start()
 
     def step(t, carry):
-        for lag, stage in ((0, pack), (2, compute), (1, pass_on), (3, add_halves), (4, combine)):
+        for lag, stage in ((0, pack), (1, pass_on), (2, add_halves), (1, compute), (3, combine)):
 
             @pl.when((t >= lag) & (t < planes + lag))
             def _(lag=lag, stage=stage):
@@ -525,7 +592,7 @@
 
         return carry
 
-    lax.fori_loop(0, planes + 4, step, 0)
+    lax.fori_loop(0, planes + 3, step, 0)
 
     answer = hidden_ref[...] + pt[z].astype(jnp.float32)
     for d in range(1, planes):
@@ -536,7 +603,6 @@
 
     for d in range(1, planes):
         to = (z + d) % planes
-        line_rows(to).wait_send()
         line_info(to).wait_send()
         line_back(to).wait_send()
 
@@ -544,6 +610,7 @@
         for j in range(1, cols):
             spread(block, (k + j) % cols).wait_send()
             give_back(block, (k + j) % cols).wait_send()
+        onward(block, lambda copy: copy.wait_send())
         forward(block).wait_send()
         half_back(block).wait_send()
         return carry
@@ -579,7 +646,7 @@
             pltpu.VMEM((planes, count, width), bf16),
             pltpu.VMEM((2 * slots, units), jnp.float32),
             dma((2,)),
-            dma((planes,)), dma((planes,)), dma((planes,)), dma((planes,)),
+            dma((planes,)), dma((planes,)), dma((planes,)), dma((planes,)), dma((planes,)),
             dma((planes, cols)), dma((planes, cols)),
             dma((planes,)), dma((planes,)), dma((planes,)), dma((planes,)),
             dma((planes, cols)), dma((planes, cols)),
@@ -615,9 +682,8 @@
 ):
     tokens_dev = ssm_values.shape[0]
     decay_rates = jnp.exp2(-decay_power.astype(jnp.float32))
-    cumulative = jnp.cumsum(-step_size * decay_rates[None, :], axis=0)
     mixed_out = mixer(
-        ssm_values, ssm_gate, write_proj, read_proj, cumulative, step_size, skip_gain, norm_gain,
+        ssm_values, ssm_gate, write_proj, read_proj, step_size, decay_rates, skip_gain, norm_gain,
         out_weight,
     )
     rows_own = tokens_dev // lax.axis_size("head")

time: 203 us -> 194 us (0.956)
  Pallas kernels: 185 us -> 179 us
    pallas_call x1, Pallas kernels: 100 us -> 93.1 us  [expert_layer(): pl.pallas_call(functools.partial(moe_kernel, planes, cols, cap), out_shap...]
    unnamed x29 -> x28, local copies, waits for them, and re-layouts: 9.07 us -> 8.25 us
where the time goes in v4:
time: 194 us; the launch traced here: 193 us
  Pallas kernels  179 us (92%)
  local copies, waits for them, and re-layouts  10.7 us (6%)
  other arithmetic  3.14 us (2%)
    pallas_call x1, Pallas kernels, expert_layer(): pl.pallas_call(functools.partial(moe_kernel, planes, cols, cap), out_shap...  93.1 us
    pallas_call x1, Pallas kernels, mixer(): pl.pallas_call(functools.partial(mixer_kernel, pairs, heads_mesh), out_sh...  85.9 us
    unnamed x28, local copies, waits for them, and re-layouts  8.25 us

profile of v4, /device:TPU:0, one launch (start us, length us, event | category | flops | bytes accessed | tf_op | source)
XLA Modules:
  0.0 193.2 jit_solution(16670791156354115342)
XLA Ops:
  0.0 0.0 copy-start
  0.0 0.0 copy-start.12
  0.0 0.8 broadcast_in_dim.43
  0.8 0.1 broadcast_in_dim_reshape.3.skip_ref
  0.9 0.7 exponential_bitcast_fusion
  1.5 0.1 copy.42.rate_ref
  1.6 0.0 copy-start.1
  1.6 1.1 copy-done.1
  2.7 1.0 copy-done.2
  3.8 0.0 copy-start.3
  3.8 1.0 copy-done.3
  4.8 0.0 copy-start.4
  4.8 0.9 copy-done.4
  5.7 0.0 copy-start.5
  5.7 0.9 copy-done.5
  6.6 0.0 copy-start.6
  6.6 0.7 copy-done.6
  7.3 0.0 copy-start.7
  7.3 0.7 copy-done.7
  8.0 0.0 copy-start.10
  8.0 85.9 %shard_map.145 = f32[8,64,384]{2,1,0:T(8,128)S(1)} custom-call(bf16[256,1024]{1,0:T(8,128)(2,1)S(1)} %copy-done.2, bf16[256,1024]{1,0:T(8,128)(2,1)S(1)} %copy-done.3, bf16[256,256]{1,0:T(8,128)(2,1)S(1)} %copy-done.4, bf16[256,256]{1,0:T(8,128)(2,1)S(1)} %copy-done.5, f32[16,256]{1,0:T(8,128)S(1)} %bitcast.45, f32[16,1]{1,0:T(8,128)S(1)} %copy.42.rate_ref, ...), custom_call_target="tpu_custom_call" | custom-call | tf_op jit(solution)/shard_map/pallas_call | solution.py:357
  94.0 0.1 slice_bitcast_fusion
  94.0 0.5 copy.43
  94.5 0.3 reshape.66
  94.7 0.0 copy-done.10
  94.8 0.2 multiply_reduce_fusion
  95.0 0.0 copy-done.12
  95.0 0.1 multiply_convert_fusion.x_ref
  95.1 0.0 copy-done
  95.1 0.0 copy-start.9
  95.1 0.2 fusion.6
  95.3 0.0 copy-done.11
  95.3 0.1 select_reduce_fusion.1
  95.4 0.1 copy.44
  95.5 0.2 eq.49
  95.7 0.9 reduce-window.6
  96.6 0.2 slice_reduce_fusion
  96.8 0.1 eq.45
  97.0 0.1 fusion.3
  97.0 0.1 reshape.68
  97.2 0.1 copy.47
  97.3 0.2 select_reduce_fusion
  97.5 0.2 fusion
  97.7 0.7 maximum_bitcast_fusion.info_ref
  98.3 0.0 copy-done.8
  98.3 0.0 copy-done.9
  98.3 93.1 %shard_map.146 = bf16[64,2688]{1,0:T(8,128)(2,1)} custom-call(bf16[64,2688]{1,0:T(8,128)(2,1)} %copy-done.9, bf16[4,128,128]{2,1,0:T(8,128)(2,1)} %maximum_bitcast_fusion.info_ref, f32[64,2688]{1,0:T(8,128)} %copy-done.8, bf16[1,928,2688]{2,1,0:T(8,128)(2,1)} %bitcast.48, bf16[1,928,2688]{2,1,0:T(8,128)(2,1)} %down_hbm.1), custom_call_target="tpu_custom_call" | custom-call | flops 10217324544 | bytes 9977856 | tf_op jit(solution)/shard_map/pallas_call | solution.py:628
  191.4 1.7 copy.57
  (10 shorter events, 0.1 us)
Async XLA Ops:
  0.0 95.1 %copy-start = (bf16[2688,16]{0,1:T(8,128)(2,1)S(1)}, bf16[2688,16]{0,1:T(8,128)(2,1)}, u32[]{:S(2)}) copy-start(bf16[2688,16]{0,1:T(8,128)(2,1)} %param.26) | copy-start | bytes 258052
  0.0 95.0 %copy-start.12 = (f32[2688]{0:T(1024)S(1)}, f32[2688]{0:T(1024)}, u32[]{:S(2)}) copy-start(f32[2688]{0:T(1024)} %param.25) | copy-start | bytes 32260
  1.6 1.1 copy-start.1
  2.7 1.0 copy-start.2
  3.8 1.0 copy-start.3
  4.8 0.9 copy-start.4
  5.7 0.9 copy-start.5
  6.6 0.7 copy-start.6
  7.3 0.7 copy-start.7
  8.0 86.7 %copy-start.10 = (bf16[64,2688]{1,0:T(8,128)(2,1)S(1)}, bf16[64,2688]{1,0:T(8,128)(2,1)}, u32[]{:S(2)}) copy-start(bf16[64,2688]{1,0:T(8,128)(2,1)} %param.24) | copy-start | bytes 1032196
  8.0 87.3 %copy-start.11 = (s32[64,6]{0,1:T(8,128)S(1)}, s32[64,6]{0,1:T(8,128)}, u32[]{:S(2)}) copy-start(s32[64,6]{0,1:T(8,128)} %param.27) | copy-start | bytes 4612
  94.9 3.4 %copy-start.8 = (f32[64,2688]{1,0:T(8,128)}, f32[64,2688]{1,0:T(8,128)S(1)}, u32[]{:S(2)}) copy-start(f32[64,2688]{1,0:T(8,128)S(1)} %get-tuple-element.6.hidden_ref) | copy-start | bytes 2064388
  95.1 3.2 %copy-start.9 = (bf16[64,2688]{1,0:T(8,128)(2,1)}, bf16[64,2688]{1,0:T(8,128)(2,1)S(1)}, u32[]{:S(2)}) copy-start(bf16[64,2688]{1,0:T(8,128)(2,1)S(1)} %multiply_convert_fusion.x_ref) | copy-start | bytes 1032196

commit v5 on v4

--- a/solution.py
+++ b/solution.py
@@ -272,8 +272,6 @@
     copies[4].wait()
     project(seq)
     for k in range(1, pairs):
-        if k > 1:
-            relay(k)
         if k == 1:
             arrived(seq + across)
             project(seq + across)
@@ -283,6 +281,8 @@
             def _(source=source):
                 project(source)
 
+        if k + 1 < pairs:
+            relay(k + 1)
         for valid, source in ((z >= k, seq - 2 * k), (z + k < pairs, seq + 2 * k)):
 
             @pl.when(valid)
@@ -386,7 +386,7 @@
             dma((size, heads_mesh)), dma((size, heads_mesh)),
         ],
         compiler_params=pltpu.CompilerParams(
-            collective_id=0, has_side_effects=True, vmem_limit_bytes=48 * 1024 * 1024
+            collective_id=0, has_side_effects=True, vmem_limit_bytes=62 * 1024 * 1024
         ),
     )(
         values, gates, writes, reads, steps.T, rates[:, None],
@@ -584,7 +584,7 @@
             line_back(block).start()
 
     def step(t, carry):
-        for lag, stage in ((0, pack), (1, pass_on), (2, add_halves), (1, compute), (3, combine)):
+        for lag, stage in ((0, pack), (1, pass_on), (2, add_halves), (3, combine), (1, compute)):
 
             @pl.when((t >= lag) & (t < planes + lag))
             def _(lag=lag, stage=stage):

time: 194 us -> 191 us (0.985)
  local copies, waits for them, and re-layouts: 10.7 us -> 6.6 us
    pallas_call x1, Pallas kernels: 85.9 us -> 79.4 us  [mixer(): pl.pallas_call(functools.partial(mixer_kernel, pairs, heads_mesh), out_sh...]
    unnamed x28 -> x14, local copies, waits for them, and re-layouts: 8.25 us -> 1.85 us
    pallas_call x1, Pallas kernels: 93.1 us -> 99.1 us  [expert_layer(): pl.pallas_call(functools.partial(moe_kernel, planes, cols, cap), out_shap...]
where the time goes in v5:
time: 191 us; the launch traced here: 189 us
  Pallas kernels  178 us (93%)
  local copies, waits for them, and re-layouts  6.6 us (3%)
  other arithmetic  3.14 us (2%)
    pallas_call x1, Pallas kernels, expert_layer(): pl.pallas_call(functools.partial(moe_kernel, planes, cols, cap), out_shap...  99.1 us
    pallas_call x1, Pallas kernels, mixer(): pl.pallas_call(functools.partial(mixer_kernel, pairs, heads_mesh), out_sh...  79.4 us

profile of v5, /device:TPU:0, one launch (start us, length us, event | category | flops | bytes accessed | tf_op | source)
XLA Modules:
  0.0 188.5 jit_solution(17744571217646677172)
XLA Ops:
  0.0 0.0 copy-start
  0.0 0.0 copy-start.3
  0.0 0.0 copy-start.5
  0.0 0.8 broadcast_in_dim.43
  0.8 0.7 broadcast_in_dim_reshape.3.skip_ref
  1.5 0.7 exponential_bitcast_fusion
  2.1 0.7 copy.42.rate_ref
  2.8 0.0 copy-start.4
  2.8 79.4 %shard_map.145 = f32[8,64,384]{2,1,0:T(8,128)} custom-call(bf16[256,1024]{1,0:T(8,128)(2,1)} %value_hbm.1, bf16[256,1024]{1,0:T(8,128)(2,1)} %gate_hbm.1, bf16[256,256]{1,0:T(8,128)(2,1)} %write_hbm.1, bf16[256,256]{1,0:T(8,128)(2,1)} %read_hbm.1, f32[16,256]{1,0:T(8,128)} %bitcast.45, f32[16,1]{1,0:T(8,128)} %copy.42.rate_ref, ...), custom_call_target="tpu_custom_call" | custom-call | tf_op jit(solution)/shard_map/pallas_call | solution.py:357
  82.2 1.2 slice_bitcast_fusion
  83.4 0.5 copy.43
  83.9 0.3 reshape.66
  84.1 0.0 copy-done.3
  84.2 0.2 multiply_reduce_fusion
  84.4 0.0 copy-start.1
  84.4 0.0 copy-done.5
  84.4 0.1 multiply_convert_fusion.x_ref
  84.5 0.0 copy-done
  84.5 0.0 copy-start.2
  84.5 0.2 fusion.6
  84.7 0.0 copy-done.4
  84.7 0.1 select_reduce_fusion.1
  84.8 0.1 copy.44
  84.9 0.2 eq.49
  85.1 0.9 reduce-window.6
  86.0 0.2 slice_reduce_fusion
  86.2 0.1 eq.45
  86.4 0.1 fusion.3
  86.5 0.1 reshape.68
  86.6 0.1 copy.47
  86.7 0.2 select_reduce_fusion
  86.9 0.2 fusion
  87.1 0.7 maximum_bitcast_fusion.info_ref
  87.7 0.0 copy-done.1
  87.7 0.0 copy-done.2
  87.7 99.1 %shard_map.146 = bf16[64,2688]{1,0:T(8,128)(2,1)} custom-call(bf16[64,2688]{1,0:T(8,128)(2,1)} %copy-done.2, bf16[4,128,128]{2,1,0:T(8,128)(2,1)} %maximum_bitcast_fusion.info_ref, f32[64,2688]{1,0:T(8,128)} %copy-done.1, bf16[1,928,2688]{2,1,0:T(8,128)(2,1)} %bitcast.48, bf16[1,928,2688]{2,1,0:T(8,128)(2,1)} %down_hbm.1), custom_call_target="tpu_custom_call" | custom-call | flops 10217324544 | bytes 9977856 | tf_op jit(solution)/shard_map/pallas_call | solution.py:628
  186.8 1.7 copy.57
  (7 shorter events, 0.1 us)
Async XLA Ops:
  0.0 84.5 %copy-start = (bf16[2688,16]{0,1:T(8,128)(2,1)S(1)}, bf16[2688,16]{0,1:T(8,128)(2,1)}, u32[]{:S(2)}) copy-start(bf16[2688,16]{0,1:T(8,128)(2,1)} %param.26) | copy-start | bytes 258052
  0.0 84.1 %copy-start.3 = (bf16[64,2688]{1,0:T(8,128)(2,1)S(1)}, bf16[64,2688]{1,0:T(8,128)(2,1)}, u32[]{:S(2)}) copy-start(bf16[64,2688]{1,0:T(8,128)(2,1)} %param.24) | copy-start | bytes 1032196
  0.0 84.4 %copy-start.5 = (f32[2688]{0:T(1024)S(1)}, f32[2688]{0:T(1024)}, u32[]{:S(2)}) copy-start(f32[2688]{0:T(1024)} %param.25) | copy-start | bytes 32260
  2.8 81.9 %copy-start.4 = (s32[64,6]{0,1:T(8,128)S(1)}, s32[64,6]{0,1:T(8,128)}, u32[]{:S(2)}) copy-start(s32[64,6]{0,1:T(8,128)} %param.27) | copy-start | bytes 4612
  84.4 3.4 %copy-start.1 = (f32[64,2688]{1,0:T(8,128)}, f32[64,2688]{1,0:T(8,128)S(1)}, u32[]{:S(2)}) copy-start(f32[64,2688]{1,0:T(8,128)S(1)} %get-tuple-element.6.hidden_ref) | copy-start | bytes 2064388
  84.5 3.2 %copy-start.2 = (bf16[64,2688]{1,0:T(8,128)(2,1)}, bf16[64,2688]{1,0:T(8,128)(2,1)S(1)}, u32[]{:S(2)}) copy-start(bf16[64,2688]{1,0:T(8,128)(2,1)S(1)} %multiply_convert_fusion.x_ref) | copy-start | bytes 1032196
